TPU v7x, 128 devices: a whole 4x4x4 slice. The times are simulated.
128 devices in a mesh: dp: 4 (over x), space: 32 (over z, y, core).
Axes of the slice: x: 4, y: 4, z: 4, core: 2. Of those that a mesh axis runs over, the one named last changes fastest.
Arguments:
- tiles: bfloat16 [4096, 32, 2048], P(('dp', 'space')), may hold values from -6 to 6
- cotangent: bfloat16 [4096, 32, 8192], P(('dp', 'space')), may hold values from -6 to 6
- neighbours: int32 [4096, 8], P(('dp', 'space')), may hold values from -1 to 1023, as said below
- conv_weight: bfloat16 [9, 4096], replicated, may hold values from -0.25 to 0.25
- expand_weight: bfloat16 [64, 256], replicated, may hold values from -0.375 to 0.375
- norm_scale: float32 [64], replicated, may hold values from 0.1 to 1.9
- norm_shift: float32 [64], replicated, may hold values from -3 to 3
Outputs:
- tile_grad: bfloat16 [4096, 32, 2048], P(('dp', 'space'))
- conv_grad: float32 [9, 4096], replicated
- expand_grad: float32 [64, 256], replicated
Inputs may be any that keep to these rules, and one draw needn't show every extreme that they name: `neighbours`: each slide's tissue tiles are listed in raster order of a grid of 23 rows and 95 columns; an entry names the tile in that grid direction, -1 where it is background or outside the grid. Relations are mutual.
All inputs are finite; a program needn't handle non-finite values.
Results may differ from a plain program's by a relative error of at most 0.0049.
Values may be sent and summed in bfloat16 or wider, within the bound.
No kernel may reach another device: no remote copies, remote signals or barrier semaphores. Data moves between devices by JAX's collectives and lax.ppermute only.
A program may use at most 256 MiB of HBM per device.

v0:
```python
import math

import jax
import jax.numpy as jnp
import numpy as np
from jax import lax
from jax.sharding import PartitionSpec as P

REACH = 3


early_dirs = np.array([0, 2, 4, 5])
late_dirs = np.array([1, 3, 6, 7])


def passed_along(value, axis, by):
    length = lax.axis_size(axis)
    pairs = [(i, i + by) for i in range(length) if 0 <= i + by < length]
    return lax.ppermute(value, axis, pairs)


def edge_parts(features):
    tile_count, tile_side, _, channels = features.shape
    bottom_row = features[:, tile_side - 1].reshape(tile_count, tile_side * channels)
    right_col = features[:, :, tile_side - 1].reshape(tile_count, tile_side * channels)
    top_row = features[:, 0].reshape(tile_count, tile_side * channels)
    left_col = features[:, :, 0].reshape(tile_count, tile_side * channels)
    return (jnp.stack([bottom_row, right_col], axis=1), jnp.stack([top_row, left_col], axis=1))


def assemble(features, early, late, early_ok, late_ok):
    tile_count, tile_side, _, channels = features.shape

    def cycle_piece(strip_rows, present):
        shaped = strip_rows.reshape(tile_count, tile_side, channels)
        return jnp.where(present[:, None, None], shaped, jnp.zeros((), features.dtype))

    north_row = cycle_piece(early[:, 0, 0], early_ok[:, 0])
    west_col = cycle_piece(early[:, 1, 1], early_ok[:, 1])
    north_west = cycle_piece(early[:, 2, 0], early_ok[:, 2])[:, tile_side - 1]
    north_east = cycle_piece(early[:, 3, 0], early_ok[:, 3])[:, 0]
    south_row = cycle_piece(late[:, 0, 0], late_ok[:, 0])
    east_col = cycle_piece(late[:, 1, 1], late_ok[:, 1])
    south_west = cycle_piece(late[:, 2, 0], late_ok[:, 2])[:, tile_side - 1]
    south_east = cycle_piece(late[:, 3, 0], late_ok[:, 3])[:, 0]
    upper_cycle = jnp.concatenate([north_west[:, None], north_row, north_east[:, None]], axis=1)
    middle = jnp.concatenate([west_col[:, :, None], features, east_col[:, :, None]], axis=2)
    lower_cycle = jnp.concatenate([south_west[:, None], south_row, south_east[:, None]], axis=1)
    return jnp.concatenate([upper_cycle[:, None], middle, lower_cycle[:, None]], axis=1)


def fetch_window(strips, direction):
    pieces = [strips]
    for distance in range(1, REACH + 1):
        pieces.append(passed_along(strips, "space", direction * distance))
    return jnp.stack(pieces, axis=0)


def halo_field(features, neighbours, position):
    tile_count = features.shape[0]
    earlier_edges, later_edges = edge_parts(features)
    strip_width = earlier_edges.shape[-1]
    early_index = neighbours[:, early_dirs]
    late_index = neighbours[:, late_dirs]
    early_clip = jnp.maximum(early_index, 0)
    late_clip = jnp.maximum(late_index, 0)
    early_pos = (position - early_clip // tile_count) * tile_count + early_clip % tile_count
    late_pos = (late_clip // tile_count - position) * tile_count + late_clip % tile_count
    window_rows = (REACH + 1) * tile_count
    early_pos = jnp.clip(early_pos, 0, window_rows - 1)
    late_pos = jnp.clip(late_pos, 0, window_rows - 1)
    low_window = fetch_window(earlier_edges, 1).reshape(window_rows, 2, strip_width)
    high_window = fetch_window(later_edges, -1).reshape(window_rows, 2, strip_width)
    early = jnp.take(low_window, early_pos, axis=0)
    late = jnp.take(high_window, late_pos, axis=0)
    return assemble(features, early, late, early_index >= 0, late_index >= 0)


def convolve(padded, kernel):
    return lax.conv_general_dilated(
        padded,
        kernel,
        (1, 1),
        "VALID",
        dimension_numbers=("NHWC", "HWIO", "NHWC"),
        preferred_element_type=jnp.float32,
    )


def kernel_grad(padded, delta_flat, tile_side, channels):
    kernel_terms = []
    for row_shift in range(3):
        for col_shift in range(3):
            window_cells = padded[
                :, row_shift : row_shift + tile_side, col_shift : col_shift + tile_side, :
            ].reshape(-1, channels)
            kernel_terms.append(
                lax.dot_general(
                    window_cells,
                    delta_flat,
                    (((0,), (0,)), ((), ())),
                    preferred_element_type=jnp.float32,
                )
            )
    return jnp.stack(kernel_terms).reshape(9, channels * channels)


def local(tiles, cotangent, neighbours, conv_weight, expand_weight, norm_scale, norm_shift):
    tile_count = tiles.shape[0]
    tile_side = tiles.shape[1]
    channels = norm_scale.shape[0]
    widened = expand_weight.shape[1]
    position = lax.axis_index("space")
    features = tiles.reshape(tile_count, tile_side, tile_side, channels)
    kernel = conv_weight.reshape(3, 3, channels, channels)
    flipped = jnp.transpose(jnp.flip(kernel, (0, 1)), (0, 1, 3, 2))
    padded = halo_field(features, neighbours, position)
    conv_out = convolve(padded, kernel)
    pre_act = conv_out * norm_scale + norm_shift
    hidden = jax.nn.silu(pre_act).astype(jnp.bfloat16)
    upstream_in = cotangent.reshape(tile_count * tile_side * tile_side, widened)
    upstream = lax.dot_general(
        upstream_in, expand_weight, (((1,), (1,)), ((), ())), preferred_element_type=jnp.float32
    )
    sigmoid_pre = jax.nn.sigmoid(pre_act)
    conv_delta = (
        upstream.reshape(pre_act.shape)
        * sigmoid_pre
        * (1.0 + pre_act * (1.0 - sigmoid_pre))
        * norm_scale
    ).astype(jnp.bfloat16)
    padded_delta = halo_field(conv_delta, neighbours, position)
    input_grad = (
        convolve(padded_delta, flipped)
        .astype(jnp.bfloat16)
        .reshape(tile_count, tile_side, tile_side * channels)
    )
    conv_local = kernel_grad(padded, conv_delta.reshape(-1, channels), tile_side, channels)
    expand_local = lax.dot_general(
        hidden.reshape(-1, channels),
        upstream_in,
        (((0,), (0,)), ((), ())),
        preferred_element_type=jnp.float32,
    )
    conv_total, expand_total = lax.psum((conv_local, expand_local), ("dp", "space"))
    cell_total = lax.axis_size("dp") * lax.axis_size("space") * tile_count * tile_side * tile_side
    loss_scale = 1.0 / math.sqrt(cell_total)
    return (input_grad, conv_total * loss_scale, expand_total * loss_scale)


def solution(mesh):
    placed = (
        P(("dp", "space"), None, None),
        P(("dp", "space"), None, None),
        P(("dp", "space"), None),
        P(),
        P(),
        P(),
        P(),
    )
    return jax.shard_map(
        local,
        mesh=mesh,
        in_specs=placed,
        out_specs=(P(("dp", "space"), None, None), P(), P()),
        check_vma=False,
    )
```

profile of v0, /device:TPU:1, one launch (start us, length us, event | category | flops | bytes accessed | tf_op | source)
XLA Modules:
  0.0 548.0 jit_solution(8928753510414764779)
XLA Ops:
  7.3 12.9 %reshape.129 = bf16[32,32,32,64]{3,2,1,0:T(8,128)(2,1)} reshape(bf16[32,32,2048]{2,1,0:T(8,128)(2,1)} %param.15) | data formatting | bytes 8388608 | tf_op jit(solution)/shard_map/reshape | solution.py:114
  21.2 5.4 slice_reduce_fusion.3
  27.2 6.2 %collective-permute-start.2 = (bf16[32,2,2048]{2,0,1:T(8,128)(2,1)S(1)}, bf16[32,2,2048]{2,0,1:T(8,128)(2,1)S(1)}, u32[]{:S(2)}, u32[]{:S(2)}) collective-permute-start(bf16[32,2,2048]{2,0,1:T(8,128)(2,1)S(1)} %constant_dynamic-update-slice_fusion), channel_id=1, source_target_pairs={{0,3},{1,4},{2,5},{3,6},{4,7},{5,8},{6,9},{7,10},{8,11},{9,12},{10... | collective-permute-start | bytes 786440 | tf_op jit(solution)/shard_map/ppermute | solution.py:19
  38.2 2.7 collective-permute-start.3
  44.0 12.9 %reshape_reshape.3 = bf16[32768,64]{1,0:T(8,128)(2,1)} reshape(bf16[32,32,2048]{2,1,0:T(8,128)(2,1)} %param.15) | data formatting | bytes 8388608 | tf_op jit(solution)/shard_map/reshape;reshape | solution.py:96
  57.3 25.7 %reshape.138 = bf16[32768,256]{1,0:T(8,128)(2,1)} reshape(bf16[32,32,8192]{2,1,0:T(8,128)(2,1)} %param.16) | data formatting | bytes 33554432 | tf_op jit(solution)/shard_map/reshape | solution.py:121
  82.9 15.6 %copy.158 = bf16[128,8,32,256]{3,2,1,0:T(8,128)(2,1)} copy(bf16[128,8,32,256]{3,1,2,0:T(8,128)(2,1)} %bitcast.165) | data formatting | bytes 33554432
  110.9 2.7 gather_fusion.3
  121.1 16.4 %copy_dynamic-update-slice_fusion = bf16[32,32,34,64]{3,0,2,1:T(8,128)(2,1)} fusion(bf16[32,32,34,64]{3,0,2,1:T(8,128)(2,1)} %copy_dynamic-update-slice_fusion.2, bf16[32,32,32,64]{3,2,1,0:T(8,128)(2,1)} %reshape.129), kind=kLoop, calls=%fused_computation.30 | loop fusion | bytes 16777216
  140.7 17.1 %fusion.3 = f32[32,32,32,64]{3,0,2,1:T(8,128)} fusion(bf16[3,3,64,64]{3,2,1,0:T(8,128)(2,1)S(1)} %reshape.132, bf16[32,1,34,64]{3,0,2,1:T(8,128)(2,1)S(1)} %copy.126, bf16[32,32,34,64]{3,0,2,1:T(8,128)(2,1)} %copy_dynamic-update-slice_fusion.1, bf16[32,1,34,64]{3,0,2,1:T(8,128)(2,1)S(1)} %copy.125), kind=kOutput, calls=%fused_computation.14 | convolution fusion | flops 2420654080 | bytes 13197312 | tf_op jit(solution)/shard_map/conv_general_dilated | solution.py:80
  157.8 19.6 %multiply_convert_fusion.1 = bf16[32,32,32,64]{3,2,1,0:T(8,128)(2,1)S(1)} fusion(f32[32,32,32,64]{3,0,2,1:T(8,128)} %fusion.3, f32[64]{0:T(128)S(1)} %copy-done.36, f32[64]{0:T(128)S(1)} %copy-done.37, bf16[64,256]{1,0:T(8,128)(2,1)S(1)} %copy-done, bf16[32,32,32,256]{3,2,1,0:T(8,128)(2,1)} %bitcast.170), kind=kOutput, calls=%fused_computation.11 | convolution fusion | flops 1098907648 | bytes 29393408 | tf_op jit(solution)/shard_map/dot_general | solution.py:122
  177.5 19.9 %fusion.47 = f32[64,64]{1,0:T(8,128)S(1)} fusion(bf16[32,32,32,64]{3,2,1,0:T(8,128)(2,1)S(1)} %multiply_convert_fusion.1, bf16[32,1,34,64]{3,0,2,1:T(8,128)(2,1)S(1)} %copy.126, bf16[32,32,34,64]{3,0,2,1:T(8,128)(2,1)} %copy_dynamic-update-slice_fusion.1), kind=kOutput, calls=%fused_computation.53 | convolution fusion | flops 277626880 | bytes 8806400 | tf_op jit(solution)/shard_map/dot_general | solution.py:98
  197.4 6.2 %fusion.44 = f32[64,64]{1,0:T(8,128)S(1)} fusion(bf16[32,32,32,64]{3,2,1,0:T(8,128)(2,1)S(1)} %multiply_convert_fusion.1, bf16[32,1,34,64]{3,0,2,1:T(8,128)(2,1)S(1)} %copy.126, bf16[32,32,34,64]{3,0,2,1:T(8,128)(2,1)S(1)} %copy-done.19), kind=kOutput, calls=%fused_computation.52 | convolution fusion | flops 277626880 | bytes 8806400 | tf_op jit(solution)/shard_map/dot_general | solution.py:98
  203.6 6.2 %fusion.41 = f32[64,64]{1,0:T(8,128)S(1)} fusion(bf16[32,32,32,64]{3,2,1,0:T(8,128)(2,1)S(1)} %multiply_convert_fusion.1, bf16[32,1,34,64]{3,0,2,1:T(8,128)(2,1)S(1)} %copy.126, bf16[32,32,34,64]{3,0,2,1:T(8,128)(2,1)S(1)} %copy-done.19), kind=kOutput, calls=%fused_computation.51 | convolution fusion | flops 277626880 | bytes 8806400 | tf_op jit(solution)/shard_map/dot_general | solution.py:98
  209.8 6.7 %fusion.38 = f32[64,64]{1,0:T(8,128)S(1)} fusion(bf16[32,32,32,64]{3,2,1,0:T(8,128)(2,1)S(1)} %multiply_convert_fusion.1, bf16[32,32,34,64]{3,0,2,1:T(8,128)(2,1)S(1)} %copy-done.19, bf16[32,1,34,64]{3,0,2,1:T(8,128)(2,1)S(1)} %copy.125), kind=kOutput, calls=%fused_computation.50 | convolution fusion | flops 277626880 | bytes 8806400 | tf_op jit(solution)/shard_map/dot_general | solution.py:98
  216.5 17.7 %fusion.35 = f32[64,64]{1,0:T(8,128)S(1)} fusion(bf16[32,32,32,64]{3,2,1,0:T(8,128)(2,1)S(1)} %multiply_convert_fusion.1, bf16[32,32,34,64]{3,0,2,1:T(8,128)(2,1)} %copy_dynamic-update-slice_fusion.1, bf16[32,1,34,64]{3,0,2,1:T(8,128)(2,1)S(1)} %copy.125), kind=kOutput, calls=%fused_computation.49 | convolution fusion | flops 277626880 | bytes 8806400 | tf_op jit(solution)/shard_map/dot_general | solution.py:98
  234.2 18.2 %fusion.32 = f32[64,64]{1,0:T(8,128)S(1)} fusion(bf16[32,32,32,64]{3,2,1,0:T(8,128)(2,1)S(1)} %multiply_convert_fusion.1, bf16[32,32,34,64]{3,0,2,1:T(8,128)(2,1)} %copy_dynamic-update-slice_fusion.1, bf16[32,1,34,64]{3,0,2,1:T(8,128)(2,1)S(1)} %copy.125), kind=kOutput, calls=%fused_computation.48 | convolution fusion | flops 277626880 | bytes 8806400 | tf_op jit(solution)/shard_map/dot_general | solution.py:98
  252.5 3.4 fusion.50
  256.0 3.7 fusion.51
  259.7 12.5 %multiply_convert_fusion = bf16[32,32,32,64]{3,2,1,0:T(8,128)(2,1)} fusion(f32[32,32,32,64]{3,0,2,1:T(8,128)} %fusion.3, f32[64]{0:T(128)S(1)} %copy-done.36, f32[64]{0:T(128)S(1)} %copy-done.37), kind=kLoop, calls=%fused_computation.10 | loop fusion | flops 14680064 | bytes 12583424 | tf_op jit(solution)/shard_map/convert_element_type | solution.py:120
  272.3 3.2 slice_reduce_fusion.1
  276.1 3.5 collective-permute-start.6
  279.6 4.3 collective-permute-start.7
  283.9 7.4 %collective-permute-start.8 = (bf16[32,2,2048]{2,0,1:T(8,128)(2,1)S(1)}, bf16[32,2,2048]{2,0,1:T(8,128)(2,1)S(1)}, u32[]{:S(2)}, u32[]{:S(2)}) collective-permute-start(bf16[32,2,2048]{2,0,1:T(8,128)(2,1)S(1)} %constant_dynamic-update-slice_fusion.4), channel_id=1, source_target_pairs={{0,3},{1,4},{2,5},{3,6},{4,7},{5,8},{6,9},{7,10},{8,11},{9,12},{10... | collective-permute-start | bytes 786440 | tf_op jit(solution)/shard_map/ppermute | solution.py:19
  292.0 8.1 %convolution_bitcast_fusion = f32[64,64]{0,1:T(8,128)S(1)} fusion(bf16[32768,64]{1,0:T(8,128)(2,1)} %bitcast.166, bf16[32768,64]{1,0:T(8,128)(2,1)} %reshape_reshape.3), kind=kOutput, calls=%fused_computation.56 | convolution fusion | flops 268435456 | bytes 8404992 | tf_op jit(solution)/shard_map/dot_general | solution.py:98
  300.8 11.1 %fusion.78 = f32[64,256]{1,0:T(8,128)} fusion(bf16[32768,64]{1,0:T(8,128)(2,1)} %bitcast.167, bf16[32768,256]{1,0:T(8,128)(2,1)} %reshape.138), kind=kOutput, calls=%fused_computation.167 | convolution fusion | flops 1073741824 | bytes 21037056 | tf_op jit(solution)/shard_map/dot_general | solution.py:139
  316.8 142.2 %all-reduce.3.cloned.1.call-done = (f32[9,4096]{1,0:T(8,128)}, f32[64,256]{1,0:T(8,128)}) async-done(((f32[9,4096]{1,0:T(8,128)}, f32[64,256]{1,0:T(8,128)}), (f32[9,4096]{1,0:T(8,128)}, f32[64,256]{1,0:T(8,128)})) %all-reduce.3.cloned.1.call-update) | async-done | bytes 213008 | tf_op jit(solution)/shard_map/psum | solution.py:145
  475.7 2.7 gather_fusion.5
  484.0 13.0 %pad_maximum_fusion = bf16[32,34,34,64]{3,2,1,0:T(8,128)(2,1)S(1)} fusion(bf16[32,1,34,64]{3,2,1,0:T(8,128)(2,1)S(1)} %maximum_bitcast_fusion.3, bf16[32,32,1,64]{3,2,1,0:T(2,128)(2,1)S(1)} %broadcast_select_fusion.4, bf16[32,32,32,64]{3,2,1,0:T(8,128)(2,1)} %copy-done.2, bf16[32,32,1,64]{3,2,1,0:T(2,128)(2,1)S(1)} %broadcast_select_fusion.6, ...), kind=kLoop, calls=%fused_computation.13 | loop fusion | flops 23674880 | bytes 9469952 | tf_op jit(solution)/shard_map/concatenate | solution.py:49
  497.0 21.7 %fusion.17 = bf16[32,32,32,64]{3,0,2,1:T(8,128)(2,1)} fusion(bf16[3,3,64,64]{3,2,1,0:T(8,128)(2,1)S(1)} %copy-done.13, bf16[32,34,34,64]{3,2,1,0:T(8,128)(2,1)S(1)} %pad_maximum_fusion), kind=kOutput, calls=%fused_computation.31 | convolution fusion | flops 2418016256 | bytes 9003008 | tf_op jit(solution)/shard_map/conv_general_dilated | solution.py:80
  518.8 9.9 %copy.139 = bf16[32,32,32,64]{3,2,1,0:T(8,128)(2,1)} copy(bf16[32,32,32,64]{3,0,2,1:T(8,128)(2,1)} %fusion.17) | data formatting | bytes 8388608 | tf_op jit(solution)/shard_map/convert_element_type | solution.py:135
  528.6 12.3 %reshape.135 = bf16[32,32,2048]{2,1,0:T(8,128)(2,1)} reshape(bf16[32,32,32,64]{3,2,1,0:T(8,128)(2,1)} %copy.139) | data formatting | bytes 8388608 | tf_op jit(solution)/shard_map/reshape | solution.py:136
  (217 shorter events, 61.3 us)
Async XLA Ops:
  7.2 150.6 %copy-start = (bf16[64,256]{1,0:T(8,128)(2,1)S(1)}, bf16[64,256]{1,0:T(8,128)(2,1)}, u32[]{:S(2)}) copy-start(bf16[64,256]{1,0:T(8,128)(2,1)} %param.19) | copy-start | bytes 98308
  7.2 451.8 %all-reduce.3.cloned.1.call-start = ((), (), s32[]{:S(2)}) async-start(), calls=%async_computation | async-start | bytes 655360 | tf_op jit(solution)/shard_map/psum | solution.py:145
  20.1 36.9 %copy-start.14 = (bf16[9,4096]{1,0:T(8,128)(2,1)S(1)}, bf16[9,4096]{1,0:T(8,128)(2,1)}, u32[]{:S(2)}) copy-start(bf16[9,4096]{1,0:T(8,128)(2,1)} %param.18) | copy-start | bytes 221188
  27.2 71.4 %collective-permute-start.2 = (bf16[32,2,2048]{2,0,1:T(8,128)(2,1)S(1)}, bf16[32,2,2048]{2,0,1:T(8,128)(2,1)S(1)}, u32[]{:S(2)}, u32[]{:S(2)}) collective-permute-start(bf16[32,2,2048]{2,0,1:T(8,128)(2,1)S(1)} %constant_dynamic-update-slice_fusion), channel_id=1, source_target_pairs={{0,3},{1,4},{2,5},{3,6},{4,7},{5,8},{6,9},{7,10},{8,11},{9,12},{10... | collective-permute-start | bytes 786440 | tf_op jit(solution)/shard_map/ppermute | solution.py:19
  33.4 66.7 %collective-permute-start = (bf16[32,2,2048]{2,0,1:T(8,128)(2,1)S(1)}, bf16[32,2,2048]{2,0,1:T(8,128)(2,1)S(1)}, u32[]{:S(2)}, u32[]{:S(2)}) collective-permute-start(bf16[32,2,2048]{2,0,1:T(8,128)(2,1)S(1)} %constant_dynamic-update-slice_fusion), channel_id=1, source_target_pairs={{0,1},{1,2},{2,3},{3,4},{4,5},{5,6},{6,7},{7,8},{8,9},{9,10},{10,1... | collective-permute-start | bytes 786440 | tf_op jit(solution)/shard_map/ppermute | solution.py:19
  35.3 64.7 %collective-permute-start.1 = (bf16[32,2,2048]{2,0,1:T(8,128)(2,1)S(1)}, bf16[32,2,2048]{2,0,1:T(8,128)(2,1)S(1)}, u32[]{:S(2)}, u32[]{:S(2)}) collective-permute-start(bf16[32,2,2048]{2,0,1:T(8,128)(2,1)S(1)} %constant_dynamic-update-slice_fusion), channel_id=1, source_target_pairs={{0,2},{1,3},{2,4},{3,5},{4,6},{5,7},{6,8},{7,9},{8,10},{9,11},{10,... | collective-permute-start | bytes 786440 | tf_op jit(solution)/shard_map/ppermute | solution.py:19
  38.2 70.3 %collective-permute-start.3 = (bf16[32,2,2048]{2,0,1:T(8,128)(2,1)S(1)}, bf16[32,2,2048]{2,0,1:T(8,128)(2,1)S(1)}, u32[]{:S(2)}, u32[]{:S(2)}) collective-permute-start(bf16[32,2,2048]{2,0,1:T(8,128)(2,1)S(1)} %constant_dynamic-update-slice_fusion.2), channel_id=1, source_target_pairs={{1,0},{2,1},{3,2},{4,3},{5,4},{6,5},{7,6},{8,7},{9,8},{10,9},{11,1... | collective-permute-start | bytes 786440 | tf_op jit(solution)/shard_map/ppermute | solution.py:19
  40.9 67.6 %collective-permute-start.4 = (bf16[32,2,2048]{2,0,1:T(8,128)(2,1)S(1)}, bf16[32,2,2048]{2,0,1:T(8,128)(2,1)S(1)}, u32[]{:S(2)}, u32[]{:S(2)}) collective-permute-start(bf16[32,2,2048]{2,0,1:T(8,128)(2,1)S(1)} %constant_dynamic-update-slice_fusion.2), channel_id=1, source_target_pairs={{2,0},{3,1},{4,2},{5,3},{6,4},{7,5},{8,6},{9,7},{10,8},{11,9},{12,... | collective-permute-start | bytes 786440 | tf_op jit(solution)/shard_map/ppermute | solution.py:19
  43.9 64.1 %copy-start.34 = (pred[32]{0:T(512)(128)(4,1)}, pred[32]{0:T(512)(128)(4,1)S(1)}, u32[]{:S(2)}) copy-start(pred[32]{0:T(512)(128)(4,1)S(1)} %get-tuple-element.36) | copy-start | bytes 100
  43.9 64.2 %copy-start.32 = (pred[32]{0:T(512)(128)(4,1)}, pred[32]{0:T(512)(128)(4,1)S(1)}, u32[]{:S(2)}) copy-start(pred[32]{0:T(512)(128)(4,1)S(1)} %get-tuple-element.34) | copy-start | bytes 100
  43.9 64.3 %copy-start.30 = (pred[32]{0:T(512)(128)(4,1)}, pred[32]{0:T(512)(128)(4,1)S(1)}, u32[]{:S(2)}) copy-start(pred[32]{0:T(512)(128)(4,1)S(1)} %get-tuple-element.37) | copy-start | bytes 100
  43.9 74.7 %copy-start.28 = (pred[32]{0:T(512)(128)(4,1)}, pred[32]{0:T(512)(128)(4,1)S(1)}, u32[]{:S(2)}) copy-start(pred[32]{0:T(512)(128)(4,1)S(1)} %get-tuple-element.35) | copy-start | bytes 100
  44.0 57.4 %copy-start.10 = (s32[1024]{0:T(1024)}, s32[1024]{0:T(1024)S(1)}, u32[]{:S(2)}) copy-start(s32[1024]{0:T(1024)S(1)} %get-tuple-element.43) | copy-start | bytes 12292
  44.0 66.9 %copy-start.8 = (s32[1024]{0:T(1024)}, s32[1024]{0:T(1024)S(1)}, u32[]{:S(2)}) copy-start(s32[1024]{0:T(1024)S(1)} %get-tuple-element.42) | copy-start | bytes 12292
  57.0 47.1 %copy-start.17 = (pred[32,4]{1,0:T(8,128)(4,1)}, pred[32,4]{1,0:T(8,128)(4,1)S(1)}, u32[]{:S(2)}) copy-start(pred[32,4]{1,0:T(8,128)(4,1)S(1)} %copy.111) | copy-start | bytes 388
  57.1 56.5 %copy-start.15 = (pred[32,4]{1,0:T(8,128)(4,1)}, pred[32,4]{1,0:T(8,128)(4,1)S(1)}, u32[]{:S(2)}) copy-start(pred[32,4]{1,0:T(8,128)(4,1)S(1)} %copy.117) | copy-start | bytes 388
  57.3 83.4 %copy-start.12 = (bf16[3,3,64,64]{3,2,1,0:T(8,128)(2,1)}, bf16[3,3,64,64]{3,2,1,0:T(8,128)(2,1)S(1)}, u32[]{:S(2)}) copy-start(bf16[3,3,64,64]{3,2,1,0:T(8,128)(2,1)S(1)} %reshape.132) | copy-start | bytes 221188
  98.6 39.6 %copy-start.20 = (pred[32]{0:T(512)(128)(4,1)}, pred[32]{0:T(512)(128)(4,1)S(1)}, u32[]{:S(2)}) copy-start(pred[32]{0:T(512)(128)(4,1)S(1)} %get-tuple-element.38) | copy-start | bytes 100
  98.6 10.0 %collective-permute-start.5 = (bf16[32,2,2048]{2,0,1:T(8,128)(2,1)S(1)}, bf16[32,2,2048]{2,0,1:T(8,128)(2,1)}, u32[]{:S(2)}, u32[]{:S(2)}) collective-permute-start(bf16[32,2,2048]{2,0,1:T(8,128)(2,1)S(1)} %constant_dynamic-update-slice_fusion.2), channel_id=1, source_target_pairs={{3,0},{4,1},{5,2},{6,3},{7,4},{8,5},{9,6},{10,7},{11,8},{12,9},{13... | collective-permute-start | bytes 786440 | tf_op jit(solution)/shard_map/ppermute | solution.py:19
  177.5 94.8 %copy-start.2 = (bf16[32,32,32,64]{3,2,1,0:T(8,128)(2,1)}, bf16[32,32,32,64]{3,2,1,0:T(8,128)(2,1)S(1)}, u32[]{:S(2)}) copy-start(bf16[32,32,32,64]{3,2,1,0:T(8,128)(2,1)S(1)} %multiply_convert_fusion.1) | copy-start | bytes 12582916
  276.1 186.1 %collective-permute-start.6 = (bf16[32,2,2048]{2,0,1:T(8,128)(2,1)S(1)}, bf16[32,2,2048]{2,0,1:T(8,128)(2,1)S(1)}, u32[]{:S(2)}, u32[]{:S(2)}) collective-permute-start(bf16[32,2,2048]{2,0,1:T(8,128)(2,1)S(1)} %constant_dynamic-update-slice_fusion.4), channel_id=1, source_target_pairs={{0,1},{1,2},{2,3},{3,4},{4,5},{5,6},{6,7},{7,8},{8,9},{9,10},{10,1... | collective-permute-start | bytes 786440 | tf_op jit(solution)/shard_map/ppermute | solution.py:19
  279.6 184.2 %collective-permute-start.7 = (bf16[32,2,2048]{2,0,1:T(8,128)(2,1)S(1)}, bf16[32,2,2048]{2,0,1:T(8,128)(2,1)S(1)}, u32[]{:S(2)}, u32[]{:S(2)}) collective-permute-start(bf16[32,2,2048]{2,0,1:T(8,128)(2,1)S(1)} %constant_dynamic-update-slice_fusion.4), channel_id=1, source_target_pairs={{0,2},{1,3},{2,4},{3,5},{4,6},{5,7},{6,8},{7,9},{8,10},{9,11},{10,... | collective-permute-start | bytes 786440 | tf_op jit(solution)/shard_map/ppermute | solution.py:19
  283.9 180.0 %collective-permute-start.8 = (bf16[32,2,2048]{2,0,1:T(8,128)(2,1)S(1)}, bf16[32,2,2048]{2,0,1:T(8,128)(2,1)S(1)}, u32[]{:S(2)}, u32[]{:S(2)}) collective-permute-start(bf16[32,2,2048]{2,0,1:T(8,128)(2,1)S(1)} %constant_dynamic-update-slice_fusion.4), channel_id=1, source_target_pairs={{0,3},{1,4},{2,5},{3,6},{4,7},{5,8},{6,9},{7,10},{8,11},{9,12},{10... | collective-permute-start | bytes 786440 | tf_op jit(solution)/shard_map/ppermute | solution.py:19
  300.8 164.3 %copy-start.11 = (s32[1024]{0:T(1024)S(1)}, s32[1024]{0:T(1024)}, u32[]{:S(2)}) copy-start(s32[1024]{0:T(1024)} %copy-done.10) | copy-start | bytes 12292
  312.0 155.9 %copy-start.18 = (pred[32,4]{1,0:T(8,128)(4,1)S(1)}, pred[32,4]{1,0:T(8,128)(4,1)}, u32[]{:S(2)}) copy-start(pred[32,4]{1,0:T(8,128)(4,1)} %copy-done.17) | copy-start | bytes 388
  312.0 159.3 %copy-start.35 = (pred[32]{0:T(512)(128)(4,1)S(1)}, pred[32]{0:T(512)(128)(4,1)}, u32[]{:S(2)}) copy-start(pred[32]{0:T(512)(128)(4,1)} %copy-done.34) | copy-start | bytes 100
  312.0 159.7 %copy-start.33 = (pred[32]{0:T(512)(128)(4,1)S(1)}, pred[32]{0:T(512)(128)(4,1)}, u32[]{:S(2)}) copy-start(pred[32]{0:T(512)(128)(4,1)} %copy-done.32) | copy-start | bytes 100
  312.0 160.1 %copy-start.31 = (pred[32]{0:T(512)(128)(4,1)S(1)}, pred[32]{0:T(512)(128)(4,1)}, u32[]{:S(2)}) copy-start(pred[32]{0:T(512)(128)(4,1)} %copy-done.30) | copy-start | bytes 100
  312.0 160.7 %copy-start.29 = (pred[32]{0:T(512)(128)(4,1)S(1)}, pred[32]{0:T(512)(128)(4,1)}, u32[]{:S(2)}) copy-start(pred[32]{0:T(512)(128)(4,1)} %copy-done.28) | copy-start | bytes 100
  313.6 159.8 %collective-permute-start.9 = (bf16[32,2,2048]{2,0,1:T(8,128)(2,1)S(1)}, bf16[32,2,2048]{2,0,1:T(8,128)(2,1)S(1)}, u32[]{:S(2)}, u32[]{:S(2)}) collective-permute-start(bf16[32,2,2048]{2,0,1:T(8,128)(2,1)S(1)} %constant_dynamic-update-slice_fusion.6), channel_id=1, source_target_pairs={{1,0},{2,1},{3,2},{4,3},{5,4},{6,5},{7,6},{8,7},{9,8},{10,9},{11,1... | collective-permute-start | bytes 786440 | tf_op jit(solution)/shard_map/ppermute | solution.py:19
  315.5 157.9 %collective-permute-start.10 = (bf16[32,2,2048]{2,0,1:T(8,128)(2,1)S(1)}, bf16[32,2,2048]{2,0,1:T(8,128)(2,1)}, u32[]{:S(2)}, u32[]{:S(2)}) collective-permute-start(bf16[32,2,2048]{2,0,1:T(8,128)(2,1)S(1)} %constant_dynamic-update-slice_fusion.6), channel_id=1, source_target_pairs={{2,0},{3,1},{4,2},{5,3},{6,4},{7,5},{8,6},{9,7},{10,8},{11,9},{12,... | collective-permute-start | bytes 786440 | tf_op jit(solution)/shard_map/ppermute | solution.py:19
  462.1 11.2 %collective-permute-start.11 = (bf16[32,2,2048]{2,0,1:T(8,128)(2,1)S(1)}, bf16[32,2,2048]{2,0,1:T(8,128)(2,1)}, u32[]{:S(2)}, u32[]{:S(2)}) collective-permute-start(bf16[32,2,2048]{2,0,1:T(8,128)(2,1)S(1)} %constant_dynamic-update-slice_fusion.6), channel_id=1, source_target_pairs={{3,0},{4,1},{5,2},{6,3},{7,4},{8,5},{9,6},{10,7},{11,8},{12,9},{13... | collective-permute-start | bytes 786440 | tf_op jit(solution)/shard_map/ppermute | solution.py:19
  (23 other events, 407.2 us)
Sparse Core Ops, SparseCore 0:
  313.7 145.2 all-reduce.2
where the time goes:
time: 558 us; the launch traced here: 548 us
  matrix products  160 us (29%)
  local copies, waits for them, and re-layouts  155 us (28%)
  waiting for transfers between devices  142 us (25%)
  other arithmetic  39.8 us (7%)
  starting transfers between devices  36 us (6%)
  between operations  15.7 us (3%)
    psum x1, waiting for transfers between devices, local(): lax.psum((conv_local, expand_local), ('dp', 'space'))  142 us
    dot_general x9, matrix products, kernel_grad(): lax.dot_general(window_cells, delta_flat, (((0,), (0,)), ((), ())), prefe...  90.2 us
    conv_general_dilated x2, matrix products, convolve(): lax.conv_general_dilated(padded, kernel, (1, 1), 'VALID', dimension_numbe...  38.9 us
    ppermute x12, starting transfers between devices, passed_along(): return lax.ppermute(value, axis, pairs)  36 us
    unnamed x91, local copies, waits for them, and re-layouts  34.8 us
    reshape x1, local copies, waits for them, and re-layouts, local(): upstream_in = cotangent.reshape(tile_count * tile_side * tile_side, widened)  25.7 us
    dot_general x1, matrix products, local(): lax.dot_general(upstream_in, expand_weight, (((1,), (1,)), ((), ())), pre...  19.6 us
    concatenate x1, other arithmetic, assemble(): jnp.concatenate([upper_cycle[:, None], middle, lower_cycle[:, None]], axi...  13 us
  transfers between devices with their start and end apart: 13, of which 1 were waited for; matrix products, arithmetic and copies ran while one was open for 18% of the time, Pallas kernels for 0%

commit v1 on v0

v1 whole, which is shorter than its diff:
```python
import math

import jax
import jax.numpy as jnp
from jax import lax
from jax.experimental import pallas as pl
from jax.experimental.pallas import tpu as pltpu
from jax.sharding import PartitionSpec as P

C = 64
CU = 256
S = 32
REACH = 3
W = S * C
GROUPS = 8
GW = W // GROUPS
KW = 2 * GW
PAIR = 2 * C
PW = W + 2 * PAIR
TB = 4
BF = jnp.bfloat16
F32 = jnp.float32
AXES = ("dp", "space")


def shifted(value, by):
    length = lax.axis_size("space")
    pairs = [(i, i + by) for i in range(length) if 0 <= i + by < length]
    return lax.ppermute(value, "space", pairs)


def one_hot(index, ok, rows):
    place = jnp.where(ok, index, -1)
    return (place[:, None] == lax.broadcasted_iota(jnp.int32, (1, rows), 1)).astype(BF)


def halo(field, neighbours, position):
    count = field.shape[0]
    rows = (REACH + 1) * count

    def side(own, column, sign, names, left_lanes, right_lanes):
        first = jnp.concatenate([own, column], axis=1)
        near = shifted(first, sign)
        far = [shifted(own, sign * d) for d in range(2, REACH + 1)]
        window = jnp.concatenate([own, near[:, :W], *far], axis=0)

        def pick(name, lanes):
            index = neighbours[:, name]
            clipped = jnp.maximum(index, 0)
            place = sign * (position - clipped // count) * count + clipped % count
            chosen = one_hot(place, index >= 0, rows)
            return jnp.dot(chosen, window[:, lanes], preferred_element_type=F32)

        middle, left, right = names
        row = jnp.concatenate(
            [pick(left, slice(W - PAIR, W)), pick(middle, slice(0, W)), pick(right, slice(0, PAIR))],
            axis=1,
        )
        return row, near[:, W:]

    north, west = side(field[:, S - 1], field[count - 1, :, W - PAIR :], 1, (0, 4, 5), None, None)
    south, east = side(field[:, 0], field[0, :, :PAIR], -1, (1, 6, 7), None, None)
    return north, south, west, east


def band(kernel):
    tall = kernel.reshape(3, 3 * C, C)
    columns = [
        jnp.pad(tall, ((0, 0), (C * (j + 1), C * (4 - j)), (0, 0))) for j in range(4)
    ]
    return jnp.concatenate(columns, axis=2).reshape(3 * KW, GW)


def stack_windows(k, field_ref, prev_ref, next_ref, north_ref, south_ref, west_ref, east_ref, nb_ref, lhs_ref):
    step = pl.program_id(0)
    steps = pl.num_programs(0)
    tile = step * TB + k
    if k > 0:
        left = field_ref[k - 1, :, W - PAIR :]
    else:
        left = jnp.where(step == 0, west_ref[...], prev_ref[0])
    if k < TB - 1:
        right = field_ref[k + 1, :, :PAIR]
    else:
        right = jnp.where(step == steps - 1, east_ref[...], next_ref[0])
    left = jnp.where(nb_ref[tile, 2] >= 0, left, jnp.zeros_like(left))
    right = jnp.where(nb_ref[tile, 3] >= 0, right, jnp.zeros_like(right))
    middle = jnp.concatenate([left, field_ref[k], right], axis=1)
    wide = middle.astype(F32)
    place = lax.broadcasted_iota(jnp.int32, (S, PW), 0)
    above = jnp.where(place == 0, north_ref[pl.ds(tile, 1), :], pltpu.roll(wide, 1, 0)).astype(BF)
    below = jnp.where(place == S - 1, south_ref[pl.ds(tile, 1), :], pltpu.roll(wide, S - 1, 0)).astype(BF)
    for a, rows in enumerate((above, middle, below)):
        for g in range(GROUPS):
            at = (k * GROUPS + g) * S
            lhs_ref[at : at + S, a * KW : (a + 1) * KW] = rows[:, g * GW : g * GW + KW]


def forward_kernel(
    nb_ref, field_ref, prev_ref, next_ref, north_ref, south_ref, west_ref, east_ref, cot_ref,
    band_ref, wide_ref, half_scale_ref, half_shift_ref, scale_ref,
    delta_ref, conv_ref, expand_ref, lhs_ref, conv_acc, expand_acc, hidden_ref, stacked_ref,
):
    step = pl.program_id(0)

    @pl.when(step == 0)
    def _():
        conv_acc[...] = jnp.zeros_like(conv_acc)
        expand_acc[...] = jnp.zeros_like(expand_acc)

    per = GROUPS * S
    for k in range(TB):
        stack_windows(k, field_ref, prev_ref, next_ref, north_ref, south_ref, west_ref, east_ref, nb_ref, lhs_ref)
    for k in range(TB):
        rows = slice(k * per, (k + 1) * per)
        conv = jnp.dot(lhs_ref[rows, :], band_ref[...], preferred_element_type=F32)
        cot = jnp.concatenate(
            [cot_ref[k, :, g * 4 * CU : (g + 1) * 4 * CU] for g in range(GROUPS)], axis=0
        )
        up = jnp.dot(cot, wide_ref[...], preferred_element_type=F32)
        half = conv * half_scale_ref[...] + half_shift_ref[...]
        th = jnp.tanh(half)
        s = 0.5 * th + 0.5
        hidden = half * (th + 1.0)
        delta = (up * scale_ref[...] * (s + hidden * (1.0 - s))).astype(BF)
        hidden_ref[rows, :] = hidden.astype(BF)
        stacked_ref[rows, :] = delta
        for g in range(GROUPS):
            delta_ref[k, :, g * GW : (g + 1) * GW] = delta[g * S : (g + 1) * S]
    contract = (((0,), (0,)), ((), ()))
    conv_acc[...] += lax.dot_general(stacked_ref[...], lhs_ref[...], contract, preferred_element_type=F32)
    total = expand_acc[...]
    for j in range(4):
        cot = jnp.concatenate(
            [
                cot_ref[k, :, (g * 4 + j) * CU : (g * 4 + j + 1) * CU]
                for k in range(TB)
                for g in range(GROUPS)
            ],
            axis=0,
        )
        total += lax.dot_general(hidden_ref[:, j * C : (j + 1) * C], cot, contract, preferred_element_type=F32)
    expand_acc[...] = total

    @pl.when(step == pl.num_programs(0) - 1)
    def _():
        expand_ref[...] = expand_acc[...]
        for a in range(3):
            for b in range(3):
                part = jnp.zeros((C, C), F32)
                for j in range(4):
                    lanes = a * KW + C * (j + b + 1)
                    part += conv_acc[j * C : (j + 1) * C, lanes : lanes + C]
                conv_ref[3 * a + b] = part.T


def backward_kernel(
    nb_ref, field_ref, prev_ref, next_ref, north_ref, south_ref, west_ref, east_ref, band_ref, out_ref, lhs_ref
):
    per = GROUPS * S
    for k in range(TB):
        stack_windows(k, field_ref, prev_ref, next_ref, north_ref, south_ref, west_ref, east_ref, nb_ref, lhs_ref)
    for k in range(TB):
        rows = slice(k * per, (k + 1) * per)
        grad = jnp.dot(lhs_ref[rows, :], band_ref[...], preferred_element_type=F32).astype(BF)
        for g in range(GROUPS):
            out_ref[k, :, g * GW : (g + 1) * GW] = grad[g * S : (g + 1) * S]


def field_specs(count):
    last = W // PAIR - 1
    return [
        pl.BlockSpec((TB, S, W), lambda i, nb: (i, 0, 0)),
        pl.BlockSpec((1, S, PAIR), lambda i, nb: (jnp.maximum(i * TB - 1, 0), 0, last)),
        pl.BlockSpec((1, S, PAIR), lambda i, nb: (jnp.minimum(i * TB + TB, count - 1), 0, 0)),
        pl.BlockSpec((count, PW), lambda i, nb: (0, 0)),
        pl.BlockSpec((count, PW), lambda i, nb: (0, 0)),
        pl.BlockSpec((S, PAIR), lambda i, nb: (0, 0)),
        pl.BlockSpec((S, PAIR), lambda i, nb: (0, 0)),
    ]


def whole(*shape):
    return pl.BlockSpec(shape, lambda i, nb: (0,) * len(shape))


def forward(tiles, halos, cotangent, neighbours, bands, wide, half_scale, half_shift, scale):
    count = tiles.shape[0]
    rows = TB * GROUPS * S
    return pl.pallas_call(
        forward_kernel,
        grid_spec=pltpu.PrefetchScalarGridSpec(
            num_scalar_prefetch=1,
            grid=(count // TB,),
            in_specs=[
                *field_specs(count),
                pl.BlockSpec((TB, S, S * CU), lambda i, nb: (i, 0, 0)),
                whole(3 * KW, GW), whole(4 * CU, GW), whole(1, GW), whole(1, GW), whole(1, GW),
            ],
            out_specs=[
                pl.BlockSpec((TB, S, W), lambda i, nb: (i, 0, 0)),
                whole(9, C, C),
                whole(C, CU),
            ],
            scratch_shapes=[
                pltpu.VMEM((rows, 3 * KW), BF),
                pltpu.VMEM((GW, 3 * KW), F32),
                pltpu.VMEM((C, CU), F32),
                pltpu.VMEM((rows, GW), BF),
                pltpu.VMEM((rows, GW), BF),
            ],
        ),
        out_shape=[
            jax.ShapeDtypeStruct((count, S, W), BF),
            jax.ShapeDtypeStruct((9, C, C), F32),
            jax.ShapeDtypeStruct((C, CU), F32),
        ],
        compiler_params=pltpu.CompilerParams(
            dimension_semantics=("arbitrary",), vmem_limit_bytes=48 * 2**20
        ),
        name="forward",
    )(neighbours, tiles, tiles, tiles, *halos, cotangent, bands, wide, half_scale, half_shift, scale)


def backward(delta, halos, neighbours, bands):
    count = delta.shape[0]
    rows = TB * GROUPS * S
    return pl.pallas_call(
        backward_kernel,
        grid_spec=pltpu.PrefetchScalarGridSpec(
            num_scalar_prefetch=1,
            grid=(count // TB,),
            in_specs=[*field_specs(count), whole(3 * KW, GW)],
            out_specs=pl.BlockSpec((TB, S, W), lambda i, nb: (i, 0, 0)),
            scratch_shapes=[pltpu.VMEM((rows, 3 * KW), BF)],
        ),
        out_shape=jax.ShapeDtypeStruct((count, S, W), BF),
        compiler_params=pltpu.CompilerParams(
            dimension_semantics=("arbitrary",), vmem_limit_bytes=48 * 2**20
        ),
        name="backward",
    )(neighbours, delta, delta, delta, *halos, bands)


def swapped(value, move):
    cells = [(x, z, y, c) for x in range(4) for z in range(4) for y in range(4) for c in range(2)]
    number = {cell: i for i, cell in enumerate(cells)}
    return lax.ppermute(value, AXES, [(number[cell], number[move(cell)]) for cell in cells])


def flip(axis, second):
    def move(cell):
        there = list(cell)
        there[axis] = 3 - cell[axis] if second else cell[axis] ^ 1
        return tuple(there)

    return move


def summed(value):
    half = value.shape[0] // 2
    even = lax.axis_index("space") % 2 == 0
    low, high = value[:half], value[half:]
    part = jnp.where(even, low, high) + swapped(jnp.where(even, high, low), flip(3, False))
    for axis in range(3):
        for second in (False, True):
            part = part + swapped(part, flip(axis, second))
    other = swapped(part, flip(3, False))
    return jnp.concatenate([jnp.where(even, part, other), jnp.where(even, other, part)], axis=0)


def local(tiles, cotangent, neighbours, conv_weight, expand_weight, norm_scale, norm_shift):
    count = tiles.shape[0]
    position = lax.axis_index("space")
    kernel = conv_weight.reshape(3, 3, C, C)
    flipped = jnp.transpose(jnp.flip(kernel, (0, 1)), (0, 1, 3, 2))
    turned = expand_weight.T
    wide = jnp.concatenate([jnp.pad(turned, ((CU * j, CU * (3 - j)), (0, 0))) for j in range(4)], axis=1)
    scale = jnp.tile(norm_scale, 4)[None]
    half_shift = 0.5 * jnp.tile(norm_shift, 4)[None]
    delta, conv_part, expand_part = forward(
        tiles, halo(tiles, neighbours, position), cotangent, neighbours, band(kernel), wide, 0.5 * scale, half_shift, scale
    )
    cells = lax.axis_size("dp") * lax.axis_size("space") * count * S * S
    part = jnp.concatenate([conv_part.reshape(9 * 32, 2 * C), expand_part.reshape(2 * C, 2 * C)], axis=0)
    total = summed(part) * (1.0 / math.sqrt(cells))
    grad = backward(delta, halo(delta, neighbours, position), neighbours, band(flipped))
    return grad, total[: 9 * 32].reshape(9, C * C), total[9 * 32 :].reshape(C, CU)


def solution(mesh):
    placed = (P(AXES, None, None), P(AXES, None, None), P(AXES, None), P(), P(), P(), P())
    return jax.shard_map(
        local,
        mesh=mesh,
        in_specs=placed,
        out_specs=(P(AXES, None, None), P(), P()),
        check_vma=False,
    )
```

time: 558 us -> 141 us (0.25); the launches traced: 548 us -> 140 us
  matrix products: 160 us -> 2.48 us
  local copies, waits for them, and re-layouts: 155 us -> 10.6 us
  waiting for transfers between devices: 142 us -> 23.2 us
  Pallas kernels: 0 us -> 40.1 us
  other arithmetic: 39.8 us -> 0.9 us
  starting transfers between devices: 36 us -> 61.7 us
  between operations: 15.7 us -> 1.18 us
    psum x1 -> x0, waiting for transfers between devices: 142 us -> none  [local(): lax.psum((conv_local, expand_local), ('dp', 'space'))]
    dot_general x11 -> x12, matrix products: 121 us -> 2.48 us  [pick(): return jnp.dot(chosen, window[:, lanes], preferred_element_type=F32)]
    reshape x8 -> x5, local copies, waits for them, and re-layouts: 55.4 us -> 1.67 us  [the longest x1 0.73 us: local(): total[:9 * 32].reshape(9, C * C)]
    pallas_call x0 -> x2, Pallas kernels: none -> 40.1 us  [the longest x1 30.3 us: forward(): pl.pallas_call(forward_kernel, grid_spec=pltpu.PrefetchScalarGridSpec(num...]
    conv_general_dilated x2 -> x0, matrix products: 38.9 us -> none  [convolve(): lax.conv_general_dilated(padded, kernel, (1, 1), 'VALID', dimension_numbe...]
    unnamed x91 -> x16, local copies, waits for them, and re-layouts: 34.8 us -> 0.38 us
    ppermute x12 -> x20, starting transfers between devices: 36 us -> 61.7 us  [the longest x12 38.4 us: shifted(): return lax.ppermute(value, 'space', pairs)]
    ppermute x12 -> x20, waiting for transfers between devices: 0.03 us -> 23.2 us  [the longest x8 16.4 us: swapped(): lax.ppermute(value, AXES, [(number[cell], number[move(cell)]) for cell in...]
  transfers between devices with their start and end apart: 13 -> 20, of which waited for: 1 -> 10; matrix products, arithmetic and copies ran while one was open for 18% -> 3% of each run, Pallas kernels for 0% -> 7%
where the time goes in v1:
time: 141 us; the launch traced here: 140 us
  starting transfers between devices  61.7 us (44%)
  Pallas kernels  40.1 us (28%)
  waiting for transfers between devices  23.2 us (16%)
  local copies, waits for them, and re-layouts  10.6 us (8%)
  matrix products  2.48 us (2%)
    ppermute x12, starting transfers between devices, shifted(): return lax.ppermute(value, 'space', pairs)  38.4 us
    pallas_call x1, Pallas kernels, forward(): pl.pallas_call(forward_kernel, grid_spec=pltpu.PrefetchScalarGridSpec(num...  30.3 us
    ppermute x8, starting transfers between devices, swapped(): lax.ppermute(value, AXES, [(number[cell], number[move(cell)]) for cell in...  23.3 us
    ppermute x8, waiting for transfers between devices, swapped(): lax.ppermute(value, AXES, [(number[cell], number[move(cell)]) for cell in...  16.4 us
    pallas_call x1, Pallas kernels, backward(): pl.pallas_call(backward_kernel, grid_spec=pltpu.PrefetchScalarGridSpec(nu...  9.85 us
    ppermute x12, waiting for transfers between devices, shifted(): return lax.ppermute(value, 'space', pairs)  6.83 us
    pallas_call x1, local copies, waits for them, and re-layouts, forward(): pl.pallas_call(forward_kernel, grid_spec=pltpu.PrefetchScalarGridSpec(num...  4.49 us
  transfers between devices with their start and end apart: 20, of which 10 were waited for; matrix products, arithmetic and copies ran while one was open for 3% of the time, Pallas kernels for 7%

profile of v1, /device:TPU:1, one launch (start us, length us, event | category | flops | bytes accessed | tf_op | source)
XLA Modules:
  0.0 140.2 jit_solution(5784934939218117060)
XLA Ops:
  0.7 2.0 %fusion.157 = (bf16[32,1,2048]{2,1,0:T(2,128)(2,1)S(1)}, bf16[32,1,2048]{2,1,0:T(2,128)(2,1)S(1)}) fusion(bf16[32,32,2048]{2,1,0:T(8,128)(2,1)} %next_ref.1), kind=kLoop, calls=%fused_computation.224 | loop fusion | bytes 524288 | tf_op jit(solution)/shard_map/slice | solution.py:62
  2.8 6.2 %collective-permute-start.2 = (bf16[32,2048]{1,0:T(8,128)(2,1)S(1)}, bf16[32,2048]{1,0:T(8,128)(2,1)S(1)}, u32[]{:S(2)}, u32[]{:S(2)}) collective-permute-start(bf16[32,2048]{1,0:T(8,128)(2,1)S(1)} %bitcast.44), channel_id=1, source_target_pairs={{0,3},{1,4},{2,5},{3,6},{4,7},{5,8},{6,9},{7,10},{8,11},{9,12},{10... | collective-permute-start | bytes 393224 | tf_op jit(solution)/shard_map/ppermute | solution.py:29
  9.0 2.3 %collective-permute-start.1 = (bf16[32,2048]{1,0:T(8,128)(2,1)S(1)}, bf16[32,2048]{1,0:T(8,128)(2,1)S(1)}, u32[]{:S(2)}, u32[]{:S(2)}) collective-permute-start(bf16[32,2048]{1,0:T(8,128)(2,1)S(1)} %bitcast.45), channel_id=1, source_target_pairs={{0,2},{1,3},{2,4},{3,5},{4,6},{5,7},{6,8},{7,9},{8,10},{9,11},{10,... | collective-permute-start | bytes 393224 | tf_op jit(solution)/shard_map/ppermute | solution.py:29
  11.5 1.3 collective-permute-start.5
  12.8 1.3 collective-permute-start.4
  14.8 3.6 %collective-permute-start = (bf16[32,2176]{1,0:T(8,128)(2,1)S(1)}, bf16[32,2176]{1,0:T(8,128)(2,1)S(1)}, u32[]{:S(2)}, u32[]{:S(2)}) collective-permute-start(bf16[32,2176]{1,0:T(8,128)(2,1)S(1)} %pad_maximum_fusion.4), channel_id=1, source_target_pairs={{0,1},{1,2},{2,3},{3,4},{4,5},{5,6},{6,7},{7,8},{8,9},{9,10},{10,1... | collective-permute-start | bytes 417800 | tf_op jit(solution)/shard_map/ppermute | solution.py:29
  20.4 1.9 %collective-permute-start.3 = (bf16[32,2176]{1,0:T(8,128)(2,1)S(1)}, bf16[32,2176]{1,0:T(8,128)(2,1)S(1)}, u32[]{:S(2)}, u32[]{:S(2)}) collective-permute-start(bf16[32,2176]{1,0:T(8,128)(2,1)S(1)} %pad_maximum_fusion.5), channel_id=1, source_target_pairs={{1,0},{2,1},{3,2},{4,3},{5,4},{6,5},{7,6},{8,7},{9,8},{10,9},{11,1... | collective-permute-start | bytes 417800 | tf_op jit(solution)/shard_map/ppermute | solution.py:29
  23.0 4.5 %collective-permute-done.3 = bf16[32,2176]{1,0:T(8,128)(2,1)S(1)} collective-permute-done((bf16[32,2176]{1,0:T(8,128)(2,1)S(1)}, bf16[32,2176]{1,0:T(8,128)(2,1)S(1)}, u32[]{:S(2)}, u32[]{:S(2)}) %collective-permute-start.3) | collective-permute-done | bytes 139296 | tf_op jit(solution)/shard_map/ppermute | solution.py:29
  28.2 30.3 %forward.1 = (bf16[32,32,2048]{2,1,0:T(8,128)(2,1)}, f32[9,64,64]{2,1,0:T(8,128)S(1)}, f32[64,256]{1,0:T(8,128)S(1)}) custom-call(s32[32,8]{1,0:T(8,128)S(1)} %copy.25.nb_ref, bf16[32,32,2048]{2,1,0:T(8,128)(2,1)} %next_ref.1, bf16[32,32,2048]{2,1,0:T(8,128)(2,1)} %next_ref.1, bf16[32,32,2048]{2,1,0:T(8,128)(2,1)} %next_ref.1, ...), custom_call_target="tpu_custom_call" | custom-call | tf_op jit(solution)/shard_map/forward/pallas_call | solution.py:190
  59.2 4.5 %copy.22 = bf16[32,32,2048]{2,0,1:T(8,128)(2,1)S(1)} copy(bf16[32,32,2048]{2,1,0:T(8,128)(2,1)} %get-tuple-element.6.field_ref.prev_ref.next_ref) | data formatting | bytes 8388608 | tf_op jit(solution)/shard_map/forward/pallas_call | solution.py:190
  63.7 1.3 collective-permute-start.11
  65.0 1.3 collective-permute-start.10
  66.3 6.4 %collective-permute-start.8 = (bf16[32,2048]{1,0:T(8,128)(2,1)S(1)}, bf16[32,2048]{1,0:T(8,128)(2,1)S(1)}, u32[]{:S(2)}, u32[]{:S(2)}) collective-permute-start(bf16[32,2048]{1,0:T(8,128)(2,1)S(1)} %get-tuple-element.12), channel_id=1, source_target_pairs={{0,3},{1,4},{2,5},{3,6},{4,7},{5,8},{6,9},{7,10},{8,11},{9,12},{10... | collective-permute-start | bytes 393224 | tf_op jit(solution)/shard_map/ppermute | solution.py:29
  72.7 4.4 %collective-permute-start.7 = (bf16[32,2048]{1,0:T(8,128)(2,1)S(1)}, bf16[32,2048]{1,0:T(8,128)(2,1)S(1)}, u32[]{:S(2)}, u32[]{:S(2)}) collective-permute-start(bf16[32,2048]{1,0:T(8,128)(2,1)S(1)} %get-tuple-element.12), channel_id=1, source_target_pairs={{0,2},{1,3},{2,4},{3,5},{4,6},{5,7},{6,8},{7,9},{8,10},{9,11},{10,... | collective-permute-start | bytes 393224 | tf_op jit(solution)/shard_map/ppermute | solution.py:29
  77.4 1.3 collective-permute-done.12
  78.7 6.5 %collective-permute-start.6 = (bf16[32,2176]{1,0:T(8,128)(2,1)S(1)}, bf16[32,2176]{1,0:T(8,128)(2,1)S(1)}, u32[]{:S(2)}, u32[]{:S(2)}) collective-permute-start(bf16[32,2176]{1,0:T(8,128)(2,1)S(1)} %pad_maximum_fusion.6), channel_id=1, source_target_pairs={{0,1},{1,2},{2,3},{3,4},{4,5},{5,6},{6,7},{7,8},{8,9},{9,10},{10,1... | collective-permute-start | bytes 417800 | tf_op jit(solution)/shard_map/ppermute | solution.py:29
  85.2 2.0 %collective-permute-done.6 = bf16[32,2176]{1,0:T(8,128)(2,1)S(1)} collective-permute-done((bf16[32,2176]{1,0:T(8,128)(2,1)S(1)}, bf16[32,2176]{1,0:T(8,128)(2,1)S(1)}, u32[]{:S(2)}, u32[]{:S(2)}) %collective-permute-start.6) | collective-permute-done | bytes 139296 | tf_op jit(solution)/shard_map/ppermute | solution.py:29
  87.1 1.9 %collective-permute-start.9 = (bf16[32,2176]{1,0:T(8,128)(2,1)S(1)}, bf16[32,2176]{1,0:T(8,128)(2,1)S(1)}, u32[]{:S(2)}, u32[]{:S(2)}) collective-permute-start(bf16[32,2176]{1,0:T(8,128)(2,1)S(1)} %pad_maximum_fusion.7), channel_id=1, source_target_pairs={{1,0},{2,1},{3,2},{4,3},{5,4},{6,5},{7,6},{8,7},{9,8},{10,9},{11,1... | collective-permute-start | bytes 417800 | tf_op jit(solution)/shard_map/ppermute | solution.py:29
  89.1 1.3 collective-permute-start.13
  90.8 2.2 %collective-permute-done.13 = f32[208,128]{1,0:T(8,128)S(1)} collective-permute-done((f32[208,128]{1,0:T(8,128)S(1)}, f32[208,128]{1,0:T(8,128)S(1)}, u32[]{:S(2)}, u32[]{:S(2)}) %collective-permute-start.13) | collective-permute-done | bytes 106528 | tf_op jit(solution)/shard_map/ppermute | solution.py:248
  93.0 2.6 %collective-permute-start.14 = (f32[208,128]{1,0:T(8,128)S(1)}, f32[208,128]{1,0:T(8,128)S(1)}, u32[]{:S(2)}, u32[]{:S(2)}) collective-permute-start(f32[208,128]{1,0:T(8,128)S(1)} %add.149), channel_id=1, source_target_pairs={{0,96},{1,97},{2,98},{3,99},{4,100},{5,101},{6,102},{7,103},{8,104... | collective-permute-start | bytes 319496 | tf_op jit(solution)/shard_map/ppermute | solution.py:248
  95.8 2.1 %collective-permute-done.14 = f32[208,128]{1,0:T(8,128)S(1)} collective-permute-done((f32[208,128]{1,0:T(8,128)S(1)}, f32[208,128]{1,0:T(8,128)S(1)}, u32[]{:S(2)}, u32[]{:S(2)}) %collective-permute-start.14) | collective-permute-done | bytes 106528 | tf_op jit(solution)/shard_map/ppermute | solution.py:248
  97.9 8.2 %collective-permute-start.15 = (f32[208,128]{1,0:T(8,128)S(1)}, f32[208,128]{1,0:T(8,128)S(1)}, u32[]{:S(2)}, u32[]{:S(2)}) collective-permute-start(f32[208,128]{1,0:T(8,128)S(1)} %add.150), channel_id=1, source_target_pairs={{0,8},{1,9},{2,10},{3,11},{4,12},{5,13},{6,14},{7,15},{8,0},{9,1},... | collective-permute-start | bytes 319496 | tf_op jit(solution)/shard_map/ppermute | solution.py:248
  106.1 2.0 %collective-permute-done.15 = f32[208,128]{1,0:T(8,128)S(1)} collective-permute-done((f32[208,128]{1,0:T(8,128)S(1)}, f32[208,128]{1,0:T(8,128)S(1)}, u32[]{:S(2)}, u32[]{:S(2)}) %collective-permute-start.15) | collective-permute-done | bytes 106528 | tf_op jit(solution)/shard_map/ppermute | solution.py:248
  108.2 3.7 %collective-permute-start.16 = (f32[208,128]{1,0:T(8,128)S(1)}, f32[208,128]{1,0:T(8,128)S(1)}, u32[]{:S(2)}, u32[]{:S(2)}) collective-permute-start(f32[208,128]{1,0:T(8,128)S(1)} %add.151), channel_id=1, source_target_pairs={{0,24},{1,25},{2,26},{3,27},{4,28},{5,29},{6,30},{7,31},{8,16},{9,... | collective-permute-start | bytes 319496 | tf_op jit(solution)/shard_map/ppermute | solution.py:248
  112.1 1.8 %collective-permute-done.16 = f32[208,128]{1,0:T(8,128)S(1)} collective-permute-done((f32[208,128]{1,0:T(8,128)S(1)}, f32[208,128]{1,0:T(8,128)S(1)}, u32[]{:S(2)}, u32[]{:S(2)}) %collective-permute-start.16) | collective-permute-done | bytes 106528 | tf_op jit(solution)/shard_map/ppermute | solution.py:248
  114.3 3.4 %collective-permute-done.17 = f32[208,128]{1,0:T(8,128)S(1)} collective-permute-done((f32[208,128]{1,0:T(8,128)S(1)}, f32[208,128]{1,0:T(8,128)S(1)}, u32[]{:S(2)}, u32[]{:S(2)}) %collective-permute-start.17) | collective-permute-done | bytes 106528 | tf_op jit(solution)/shard_map/ppermute | solution.py:248
  117.6 1.1 collective-permute-start.18
  118.9 3.6 %collective-permute-done.18 = f32[208,128]{1,0:T(8,128)S(1)} collective-permute-done((f32[208,128]{1,0:T(8,128)S(1)}, f32[208,128]{1,0:T(8,128)S(1)}, u32[]{:S(2)}, u32[]{:S(2)}) %collective-permute-start.18) | collective-permute-done | bytes 106528 | tf_op jit(solution)/shard_map/ppermute | solution.py:248
  122.5 6.3 %collective-permute-start.19 = (f32[208,128]{1,0:T(8,128)S(1)}, f32[208,128]{1,0:T(8,128)S(1)}, u32[]{:S(2)}, u32[]{:S(2)}) collective-permute-start(f32[208,128]{1,0:T(8,128)S(1)} %add.154), channel_id=1, source_target_pairs={{0,1},{1,0},{2,3},{3,2},{4,5},{5,4},{6,7},{7,6},{8,9},{9,8},{10,11... | collective-permute-start | bytes 319496 | tf_op jit(solution)/shard_map/ppermute | solution.py:248
  128.9 9.8 %backward.1 = bf16[32,32,2048]{2,1,0:T(8,128)(2,1)} custom-call(s32[32,8]{1,0:T(8,128)S(1)} %copy.25.nb_ref, bf16[32,32,2048]{2,1,0:T(8,128)(2,1)S(1)} %copy-done, bf16[32,32,2048]{2,1,0:T(8,128)(2,1)S(1)} %copy-done, bf16[32,32,2048]{2,1,0:T(8,128)(2,1)S(1)} %copy-done, f32[32,2304]{1,0:T(8,128)S(1)} %pad_maximum_fusion.2.north_ref, ...), custom_call_target="tpu_custom_call" | custom-call | tf_op jit(solution)/shard_map/backward/pallas_call | solution.py:228
  139.5 0.7 reshape.64
  (89 shorter events, 7.3 us)
Async XLA Ops:
  0.6 17.7 %copy-start.3 = (s32[32,8]{0,1:T(8,128)S(1)}, s32[32,8]{0,1:T(8,128)}, u32[]{:S(2)}) copy-start(s32[32,8]{0,1:T(8,128)} %param.9) | copy-start | bytes 3076
  0.6 17.8 %copy-start.1 = (bf16[9,4096]{1,0:T(8,128)(2,1)S(1)}, bf16[9,4096]{1,0:T(8,128)(2,1)}, u32[]{:S(2)}) copy-start(bf16[9,4096]{1,0:T(8,128)(2,1)} %param.10) | copy-start | bytes 221188
  0.7 18.2 %copy-start.5 = (f32[64]{0:T(128)S(1)}, f32[64]{0:T(128)}, u32[]{:S(2)}) copy-start(f32[64]{0:T(128)} %param.13) | copy-start | bytes 772
  0.7 18.3 %copy-start.4 = (f32[64]{0:T(128)S(1)}, f32[64]{0:T(128)}, u32[]{:S(2)}) copy-start(f32[64]{0:T(128)} %param.12) | copy-start | bytes 772
  0.7 18.4 %copy-start.2 = (bf16[64,256]{1,0:T(8,128)(2,1)S(1)}, bf16[64,256]{1,0:T(8,128)(2,1)}, u32[]{:S(2)}) copy-start(bf16[64,256]{1,0:T(8,128)(2,1)} %param.11) | copy-start | bytes 98308
  2.8 19.5 %collective-permute-start.2 = (bf16[32,2048]{1,0:T(8,128)(2,1)S(1)}, bf16[32,2048]{1,0:T(8,128)(2,1)S(1)}, u32[]{:S(2)}, u32[]{:S(2)}) collective-permute-start(bf16[32,2048]{1,0:T(8,128)(2,1)S(1)} %bitcast.44), channel_id=1, source_target_pairs={{0,3},{1,4},{2,5},{3,6},{4,7},{5,8},{6,9},{7,10},{8,11},{9,12},{10... | collective-permute-start | bytes 393224 | tf_op jit(solution)/shard_map/ppermute | solution.py:29
  9.0 13.3 %collective-permute-start.1 = (bf16[32,2048]{1,0:T(8,128)(2,1)S(1)}, bf16[32,2048]{1,0:T(8,128)(2,1)S(1)}, u32[]{:S(2)}, u32[]{:S(2)}) collective-permute-start(bf16[32,2048]{1,0:T(8,128)(2,1)S(1)} %bitcast.45), channel_id=1, source_target_pairs={{0,2},{1,3},{2,4},{3,5},{4,6},{5,7},{6,8},{7,9},{8,10},{9,11},{10,... | collective-permute-start | bytes 393224 | tf_op jit(solution)/shard_map/ppermute | solution.py:29
  11.5 16.0 %collective-permute-start.5 = (bf16[32,2048]{1,0:T(8,128)(2,1)S(1)}, bf16[32,2048]{1,0:T(8,128)(2,1)S(1)}, u32[]{:S(2)}, u32[]{:S(2)}) collective-permute-start(bf16[32,2048]{1,0:T(8,128)(2,1)S(1)} %bitcast.38), channel_id=1, source_target_pairs={{3,0},{4,1},{5,2},{6,3},{7,4},{8,5},{9,6},{10,7},{11,8},{12,9},{13... | collective-permute-start | bytes 393224 | tf_op jit(solution)/shard_map/ppermute | solution.py:29
  12.8 14.7 %collective-permute-start.4 = (bf16[32,2048]{1,0:T(8,128)(2,1)S(1)}, bf16[32,2048]{1,0:T(8,128)(2,1)S(1)}, u32[]{:S(2)}, u32[]{:S(2)}) collective-permute-start(bf16[32,2048]{1,0:T(8,128)(2,1)S(1)} %bitcast.39), channel_id=1, source_target_pairs={{2,0},{3,1},{4,2},{5,3},{6,4},{7,5},{8,6},{9,7},{10,8},{11,9},{12,... | collective-permute-start | bytes 393224 | tf_op jit(solution)/shard_map/ppermute | solution.py:29
  14.8 5.6 %collective-permute-start = (bf16[32,2176]{1,0:T(8,128)(2,1)S(1)}, bf16[32,2176]{1,0:T(8,128)(2,1)S(1)}, u32[]{:S(2)}, u32[]{:S(2)}) collective-permute-start(bf16[32,2176]{1,0:T(8,128)(2,1)S(1)} %pad_maximum_fusion.4), channel_id=1, source_target_pairs={{0,1},{1,2},{2,3},{3,4},{4,5},{5,6},{6,7},{7,8},{8,9},{9,10},{10,1... | collective-permute-start | bytes 417800 | tf_op jit(solution)/shard_map/ppermute | solution.py:29
  20.4 7.1 %collective-permute-start.3 = (bf16[32,2176]{1,0:T(8,128)(2,1)S(1)}, bf16[32,2176]{1,0:T(8,128)(2,1)S(1)}, u32[]{:S(2)}, u32[]{:S(2)}) collective-permute-start(bf16[32,2176]{1,0:T(8,128)(2,1)S(1)} %pad_maximum_fusion.5), channel_id=1, source_target_pairs={{1,0},{2,1},{3,2},{4,3},{5,4},{6,5},{7,6},{8,7},{9,8},{10,9},{11,1... | collective-permute-start | bytes 417800 | tf_op jit(solution)/shard_map/ppermute | solution.py:29
  63.7 48.2 %collective-permute-start.11 = (bf16[32,2048]{1,0:T(8,128)(2,1)S(1)}, bf16[32,2048]{1,0:T(8,128)(2,1)S(1)}, u32[]{:S(2)}, u32[]{:S(2)}) collective-permute-start(bf16[32,2048]{1,0:T(8,128)(2,1)S(1)} %get-tuple-element.11), channel_id=1, source_target_pairs={{3,0},{4,1},{5,2},{6,3},{7,4},{8,5},{9,6},{10,7},{11,8},{12,9},{13... | collective-permute-start | bytes 393224 | tf_op jit(solution)/shard_map/ppermute | solution.py:29
  65.0 46.9 %collective-permute-start.10 = (bf16[32,2048]{1,0:T(8,128)(2,1)S(1)}, bf16[32,2048]{1,0:T(8,128)(2,1)S(1)}, u32[]{:S(2)}, u32[]{:S(2)}) collective-permute-start(bf16[32,2048]{1,0:T(8,128)(2,1)S(1)} %get-tuple-element.11), channel_id=1, source_target_pairs={{2,0},{3,1},{4,2},{5,3},{6,4},{7,5},{8,6},{9,7},{10,8},{11,9},{12,... | collective-permute-start | bytes 393224 | tf_op jit(solution)/shard_map/ppermute | solution.py:29
  66.3 22.8 %collective-permute-start.8 = (bf16[32,2048]{1,0:T(8,128)(2,1)S(1)}, bf16[32,2048]{1,0:T(8,128)(2,1)S(1)}, u32[]{:S(2)}, u32[]{:S(2)}) collective-permute-start(bf16[32,2048]{1,0:T(8,128)(2,1)S(1)} %get-tuple-element.12), channel_id=1, source_target_pairs={{0,3},{1,4},{2,5},{3,6},{4,7},{5,8},{6,9},{7,10},{8,11},{9,12},{10... | collective-permute-start | bytes 393224 | tf_op jit(solution)/shard_map/ppermute | solution.py:29
  72.7 17.7 %collective-permute-start.7 = (bf16[32,2048]{1,0:T(8,128)(2,1)S(1)}, bf16[32,2048]{1,0:T(8,128)(2,1)S(1)}, u32[]{:S(2)}, u32[]{:S(2)}) collective-permute-start(bf16[32,2048]{1,0:T(8,128)(2,1)S(1)} %get-tuple-element.12), channel_id=1, source_target_pairs={{0,2},{1,3},{2,4},{3,5},{4,6},{5,7},{6,8},{7,9},{8,10},{9,11},{10,... | collective-permute-start | bytes 393224 | tf_op jit(solution)/shard_map/ppermute | solution.py:29
  77.3 1.4 collective-permute-start.12
  78.7 8.5 %collective-permute-start.6 = (bf16[32,2176]{1,0:T(8,128)(2,1)S(1)}, bf16[32,2176]{1,0:T(8,128)(2,1)S(1)}, u32[]{:S(2)}, u32[]{:S(2)}) collective-permute-start(bf16[32,2176]{1,0:T(8,128)(2,1)S(1)} %pad_maximum_fusion.6), channel_id=1, source_target_pairs={{0,1},{1,2},{2,3},{3,4},{4,5},{5,6},{6,7},{7,8},{8,9},{9,10},{10,1... | collective-permute-start | bytes 417800 | tf_op jit(solution)/shard_map/ppermute | solution.py:29
  87.1 19.0 %collective-permute-start.9 = (bf16[32,2176]{1,0:T(8,128)(2,1)S(1)}, bf16[32,2176]{1,0:T(8,128)(2,1)S(1)}, u32[]{:S(2)}, u32[]{:S(2)}) collective-permute-start(bf16[32,2176]{1,0:T(8,128)(2,1)S(1)} %pad_maximum_fusion.7), channel_id=1, source_target_pairs={{1,0},{2,1},{3,2},{4,3},{5,4},{6,5},{7,6},{8,7},{9,8},{10,9},{11,1... | collective-permute-start | bytes 417800 | tf_op jit(solution)/shard_map/ppermute | solution.py:29
  89.1 3.9 %collective-permute-start.13 = (f32[208,128]{1,0:T(8,128)S(1)}, f32[208,128]{1,0:T(8,128)S(1)}, u32[]{:S(2)}, u32[]{:S(2)}) collective-permute-start(f32[208,128]{1,0:T(8,128)S(1)} %select_add_fusion), channel_id=1, source_target_pairs={{0,32},{1,33},{2,34},{3,35},{4,36},{5,37},{6,38},{7,39},{8,40},{9,... | collective-permute-start | bytes 319496 | tf_op jit(solution)/shard_map/ppermute | solution.py:248
  93.0 4.8 %collective-permute-start.14 = (f32[208,128]{1,0:T(8,128)S(1)}, f32[208,128]{1,0:T(8,128)S(1)}, u32[]{:S(2)}, u32[]{:S(2)}) collective-permute-start(f32[208,128]{1,0:T(8,128)S(1)} %add.149), channel_id=1, source_target_pairs={{0,96},{1,97},{2,98},{3,99},{4,100},{5,101},{6,102},{7,103},{8,104... | collective-permute-start | bytes 319496 | tf_op jit(solution)/shard_map/ppermute | solution.py:248
  97.9 10.3 %collective-permute-start.15 = (f32[208,128]{1,0:T(8,128)S(1)}, f32[208,128]{1,0:T(8,128)S(1)}, u32[]{:S(2)}, u32[]{:S(2)}) collective-permute-start(f32[208,128]{1,0:T(8,128)S(1)} %add.150), channel_id=1, source_target_pairs={{0,8},{1,9},{2,10},{3,11},{4,12},{5,13},{6,14},{7,15},{8,0},{9,1},... | collective-permute-start | bytes 319496 | tf_op jit(solution)/shard_map/ppermute | solution.py:248
  108.2 5.8 %collective-permute-start.16 = (f32[208,128]{1,0:T(8,128)S(1)}, f32[208,128]{1,0:T(8,128)S(1)}, u32[]{:S(2)}, u32[]{:S(2)}) collective-permute-start(f32[208,128]{1,0:T(8,128)S(1)} %add.151), channel_id=1, source_target_pairs={{0,24},{1,25},{2,26},{3,27},{4,28},{5,29},{6,30},{7,31},{8,16},{9,... | collective-permute-start | bytes 319496 | tf_op jit(solution)/shard_map/ppermute | solution.py:248
  111.9 17.0 %copy-start = (bf16[32,32,2048]{2,1,0:T(8,128)(2,1)S(1)}, bf16[32,32,2048]{2,1,0:T(8,128)(2,1)}, u32[]{:S(2)}) copy-start(bf16[32,32,2048]{2,1,0:T(8,128)(2,1)} %get-tuple-element.6.field_ref.prev_ref.next_ref) | copy-start | bytes 12582916
  114.0 3.6 %collective-permute-start.17 = (f32[208,128]{1,0:T(8,128)S(1)}, f32[208,128]{1,0:T(8,128)S(1)}, u32[]{:S(2)}, u32[]{:S(2)}) collective-permute-start(f32[208,128]{1,0:T(8,128)S(1)} %add.152), channel_id=1, source_target_pairs={{0,2},{1,3},{2,0},{3,1},{4,6},{5,7},{6,4},{7,5},{8,10},{9,11},{10,... | collective-permute-start | bytes 319496 | tf_op jit(solution)/shard_map/ppermute | solution.py:248
  117.6 4.8 %collective-permute-start.18 = (f32[208,128]{1,0:T(8,128)S(1)}, f32[208,128]{1,0:T(8,128)S(1)}, u32[]{:S(2)}, u32[]{:S(2)}) collective-permute-start(f32[208,128]{1,0:T(8,128)S(1)} %add.153), channel_id=1, source_target_pairs={{0,6},{1,7},{2,4},{3,5},{4,2},{5,3},{6,0},{7,1},{8,14},{9,15},{10,... | collective-permute-start | bytes 319496 | tf_op jit(solution)/shard_map/ppermute | solution.py:248
  122.5 16.2 %collective-permute-start.19 = (f32[208,128]{1,0:T(8,128)S(1)}, f32[208,128]{1,0:T(8,128)S(1)}, u32[]{:S(2)}, u32[]{:S(2)}) collective-permute-start(f32[208,128]{1,0:T(8,128)S(1)} %add.154), channel_id=1, source_target_pairs={{0,1},{1,0},{2,3},{3,2},{4,5},{5,4},{6,7},{7,6},{8,9},{9,8},{10,11... | collective-permute-start | bytes 319496 | tf_op jit(solution)/shard_map/ppermute | solution.py:248

commit v2 on v1

v2 whole, which is shorter than its diff:
```python
import functools
import math

import jax
import jax.numpy as jnp
from jax import lax
from jax.experimental import pallas as pl
from jax.experimental.pallas import tpu as pltpu
from jax.sharding import PartitionSpec as P

C = 64
CU = 256
S = 32
REACH = 3
W = S * C
GROUPS = 8
GW = W // GROUPS
KW = 2 * GW
PAIR = 2 * C
PW = W + 2 * PAIR
TB = 4
PIECES = 4
BF = jnp.bfloat16
F32 = jnp.float32
AXES = ("dp", "space")


def shifted(value, by):
    length = lax.axis_size("space")
    pairs = [(i, i + by) for i in range(length) if 0 <= i + by < length]
    return lax.ppermute(value, "space", pairs)


def one_hot(index, ok, rows):
    place = jnp.where(ok, index, -1)
    return (place[:, None] == lax.broadcasted_iota(jnp.int32, (1, rows), 1)).astype(BF)


def halo_near(down, up):
    return shifted(down, 1), shifted(up, -1)


def halo_far(down, up, near):
    return shifted(jnp.concatenate([down, near[0]], axis=0), 2), shifted(jnp.concatenate([up, near[1]], axis=0), -2)


def halo(down, up, near, far, neighbours, position):
    count = down.shape[0]
    rows = (REACH + 1) * count

    def side(own, near, far, sign, names):
        window = jnp.concatenate([own, near, far], axis=0)

        def pick(name, lanes):
            index = neighbours[:, name]
            clipped = jnp.maximum(index, 0)
            place = sign * (position - clipped // count) * count + clipped % count
            chosen = one_hot(place, index >= 0, rows)
            return jnp.dot(chosen, window[:, lanes], preferred_element_type=F32)

        middle, left, right = names
        row = jnp.concatenate(
            [pick(left, slice(W - PAIR, W)), pick(middle, slice(0, W)), pick(right, slice(0, PAIR))],
            axis=1,
        )
        return row, near[:, W:]

    north, west = side(down, near[0], far[0], 1, (0, 4, 5))
    south, east = side(up, near[1], far[1], -1, (1, 6, 7))
    return north, south, west, east


def band(kernel):
    tall = kernel.reshape(3, 3 * C, C)
    columns = [
        jnp.pad(tall, ((0, 0), (C * (j + 1), C * (4 - j)), (0, 0))) for j in range(4)
    ]
    return jnp.concatenate(columns, axis=2).reshape(3 * KW, GW)


def store_taps(lhs_ref, at, taps):
    for a, rows in enumerate(taps):
        for g in range(GROUPS):
            lhs_ref[at + g * S : at + (g + 1) * S, a * KW : (a + 1) * KW] = rows[:, g * GW : g * GW + KW]


def kept(ok, value):
    return jnp.where(ok, value, jnp.zeros_like(value))


def with_halo(wide, north, south):
    place = lax.broadcasted_iota(jnp.int32, wide.shape, 0)
    above = jnp.where(place == 0, north, pltpu.roll(wide, 1, 0)).astype(BF)
    below = jnp.where(place == S - 1, south, pltpu.roll(wide, S - 1, 0)).astype(BF)
    return above, wide.astype(BF), below


def activate(conv, up, half_scale, half_shift, scale):
    half = conv * half_scale + half_shift
    th = jnp.tanh(half)
    s = 0.5 * th + 0.5
    hidden = half * (th + 1.0)
    return hidden, up * scale * (s + hidden * (1.0 - s))


CONTRACT = (((0,), (0,)), ((), ()))


def add_conv(acc_ref, taps, delta):
    acc_ref[...] += lax.dot_general(taps, delta, CONTRACT, preferred_element_type=F32)


def finish_conv(acc_ref, before_ref, out_ref):
    for a in range(3):
        for b in range(3):
            part = before_ref[3 * a + b]
            for j in range(4):
                at = a * KW + C * (j + b + 1)
                part += acc_ref[at : at + C, j * C : (j + 1) * C]
            out_ref[3 * a + b] = part


def forward_kernel(
    base, nb_ref, field_ref, prev_ref, next_ref, cot_ref, band_ref, wide_ref, half_scale_ref, half_shift_ref, scale_ref,
    conv_in_ref, expand_in_ref, *rest,
):
    delta_ref, rows_ref, cot_rows_ref, conv_ref, expand_ref, lhs_ref, conv_acc, expand_acc, hidden_ref, stacked_ref = rest[-10:]
    step = pl.program_id(0)
    count = nb_ref.shape[0]

    @pl.when(step == 0)
    def _():
        conv_acc[...] = jnp.zeros_like(conv_acc)
        expand_acc[...] = expand_in_ref[...]

    per = GROUPS * S
    for k in range(TB):
        tile = (step + base) * TB + k
        left = field_ref[k - 1, :, W - PAIR :] if k > 0 else prev_ref[0]
        right = field_ref[k + 1, :, :PAIR] if k < TB - 1 else next_ref[0]
        left = kept(nb_ref[tile, 2] >= 0, left)
        right = kept(nb_ref[tile, 3] >= 0, right)
        middle = jnp.concatenate([left, field_ref[k], right], axis=1)
        wide = middle.astype(F32)
        store_taps(
            lhs_ref, k * per, (pltpu.roll(wide, 1, 0).astype(BF), middle, pltpu.roll(wide, S - 1, 0).astype(BF))
        )
        place = step * TB + k
        for r, at in enumerate((0, 1, S - 2, S - 1)):
            rows_ref[r, pl.ds(place, 1), :] = wide[at : at + 1]
        cot_rows_ref[0, pl.ds(place, 1), :] = cot_ref[k, :16].astype(F32)[:1]
        cot_rows_ref[1, pl.ds(place, 1), :] = cot_ref[k, 16:].astype(F32)[15:]
    inside = lax.broadcasted_iota(jnp.int32, (per, GW), 0) & (S - 1)
    inside = (inside > 0) & (inside < S - 1)
    for k in range(TB):
        tile = (step + base) * TB + k
        rows = slice(k * per, (k + 1) * per)
        conv = jnp.dot(lhs_ref[rows, :], band_ref[...], preferred_element_type=F32)
        cot = jnp.concatenate(
            [cot_ref[k, :, g * 4 * CU : (g + 1) * 4 * CU] for g in range(GROUPS)], axis=0
        )
        up = jnp.dot(cot, wide_ref[...], preferred_element_type=F32)
        hidden, delta = activate(conv, up, half_scale_ref[...], half_shift_ref[...], scale_ref[...])
        ok = inside
        if k in (0, TB - 1):
            ok = inside & ((tile > 0) & (tile < count - 1))
        hidden_ref[rows, :] = kept(ok, hidden).astype(BF)
        delta = kept(ok, delta).astype(BF)
        stacked_ref[rows, :] = delta
        for g in range(GROUPS):
            delta_ref[k, :, g * GW : (g + 1) * GW] = delta[g * S : (g + 1) * S]
    add_conv(conv_acc, lhs_ref[...], stacked_ref[...])
    total = expand_acc[...]
    for j in range(4):
        cot = jnp.concatenate(
            [
                cot_ref[k, :, (g * 4 + j) * CU : (g * 4 + j + 1) * CU]
                for k in range(TB)
                for g in range(GROUPS)
            ],
            axis=0,
        )
        total += lax.dot_general(hidden_ref[:, j * C : (j + 1) * C], cot, CONTRACT, preferred_element_type=F32)
    expand_acc[...] = total

    @pl.when(step == pl.num_programs(0) - 1)
    def _():
        expand_ref[...] = expand_acc[...]
        finish_conv(conv_acc, conv_in_ref, conv_ref)


def edge_kernel(
    nb_ref, tile_ref, prev_ref, next_ref, cot_ref, rows_a_ref, rows_b_ref, cot_a_ref, cot_b_ref,
    north_ref, south_ref, west_ref, east_ref, band_ref, wide_ref, half_scale_ref, half_shift_ref, scale_ref,
    conv_in_ref, expand_in_ref, delta_in_ref,
    delta_ref, up_ref, down_ref, up_own_ref, down_own_ref, conv_ref, expand_ref,
    lhs_ref, cots_ref, conv_acc, expand_acc,
):
    step = pl.program_id(0)
    count = nb_ref.shape[0]
    west = kept(nb_ref[0, 2] >= 0, west_ref[...].astype(F32))
    east = kept(nb_ref[count - 1, 3] >= 0, east_ref[...].astype(F32))

    @pl.when(step == 0)
    def _():
        conv_acc[...] = jnp.zeros_like(conv_acc)
        expand_acc[...] = expand_in_ref[...]

    @pl.when(step < 2)
    def _():
        first = step == 0
        left = jnp.where(first, west, kept(nb_ref[count - 1, 2] >= 0, prev_ref[0].astype(F32)))
        right = jnp.where(first, kept(nb_ref[0, 3] >= 0, next_ref[0].astype(F32)), east)
        wide = jnp.concatenate([left, tile_ref[0].astype(F32), right], axis=1)
        north = jnp.where(first, north_ref[:1], north_ref[count - 1 :])
        south = jnp.where(first, south_ref[:1], south_ref[count - 1 :])
        store_taps(lhs_ref, 0, with_halo(wide, north, south))
        for g in range(GROUPS):
            cots_ref[g * S : (g + 1) * S, :] = cot_ref[0, :, g * 4 * CU : (g + 1) * 4 * CU]

    top = step == 2

    @pl.when(step >= 2)
    def _():
        tile_at = lax.broadcasted_iota(jnp.int32, (count, PAIR), 0)

        def row(r, at):
            found = jnp.concatenate([rows_a_ref[r], rows_b_ref[r]], axis=0)
            left = jnp.where(tile_at == 0, west[at : at + 1], found[:, :PAIR])
            right = jnp.where(tile_at == count - 1, east[at : at + 1], found[:, PW - PAIR :])
            return jnp.concatenate([left, found[:, PAIR : PW - PAIR], right], axis=1)

        edge = jnp.where(top, row(0, 0), row(3, S - 1))
        inner = jnp.where(top, row(1, 1), row(2, S - 2))
        above = jnp.where(top, north_ref[...], inner)
        below = jnp.where(top, inner, south_ref[...])
        store_taps(lhs_ref, 0, (above.astype(BF), edge.astype(BF), below.astype(BF)))
        cot = jnp.where(
            top,
            jnp.concatenate([cot_a_ref[0], cot_b_ref[0]], axis=0),
            jnp.concatenate([cot_a_ref[1], cot_b_ref[1]], axis=0),
        ).astype(BF)
        for g in range(GROUPS):
            cots_ref[g * S : (g + 1) * S, :] = cot[:, g * 4 * CU : (g + 1) * 4 * CU]

    conv = jnp.dot(lhs_ref[...], band_ref[...], preferred_element_type=F32)
    up = jnp.dot(cots_ref[...], wide_ref[...], preferred_element_type=F32)
    hidden, delta = activate(conv, up, half_scale_ref[...], half_shift_ref[...], scale_ref[...])
    at = lax.broadcasted_iota(jnp.int32, hidden.shape, 0) & (S - 1)
    ok = ((at > 0) & (at < count - 1)) | (step < 2)
    rounded = delta.astype(BF)
    hidden = kept(ok, hidden).astype(BF)
    add_conv(conv_acc, lhs_ref[...], kept(ok, delta).astype(BF))
    for j in range(4):
        expand_acc[...] += lax.dot_general(
            hidden[:, j * C : (j + 1) * C], cots_ref[:, j * CU : (j + 1) * CU], CONTRACT, preferred_element_type=F32
        )

    @pl.when(step < 2)
    def _():
        for g in range(GROUPS):
            delta_ref[0, :, g * GW : (g + 1) * GW] = rounded[g * S : (g + 1) * S]

    @pl.when(step == 0)
    def _():
        up_ref[:, W:] = rounded[:S, :PAIR]

    @pl.when(step == 1)
    def _():
        down_ref[:, W:] = rounded[(GROUPS - 1) * S :, GW - PAIR :]

    def rows_out(sent_ref, own_ref):
        for g in range(GROUPS):
            sent_ref[:, g * GW : (g + 1) * GW] = rounded[g * S : (g + 1) * S]
            own_ref[:, g * GW : (g + 1) * GW] = rounded[g * S : (g + 1) * S].astype(F32)

    @pl.when(step == 2)
    def _():
        rows_out(up_ref, up_own_ref)

    @pl.when(step == 3)
    def _():
        rows_out(down_ref, down_own_ref)
        expand_ref[...] = expand_acc[...]
        finish_conv(conv_acc, conv_in_ref, conv_ref)


def backward_kernel(
    base, nb_ref, field_ref, prev_ref, next_ref, north_ref, south_ref, west_ref, east_ref, top_ref, bottom_ref, band_ref, *rest
):
    out_ref, lhs_ref = rest[-2:]
    step = pl.program_id(0) + base
    count = nb_ref.shape[0]
    per = GROUPS * S

    def mended(value, tile, lanes):
        place = lax.broadcasted_iota(jnp.int32, value.shape, 0)
        value = jnp.where(place == 0, top_ref[pl.ds(tile, 1), :][:, lanes], value.astype(F32))
        return jnp.where(place == S - 1, bottom_ref[pl.ds(tile, 1), :][:, lanes], value)

    for k in range(TB):
        tile = step * TB + k
        left = field_ref[k - 1, :, W - PAIR :] if k > 0 else prev_ref[0]
        right = field_ref[k + 1, :, :PAIR] if k < TB - 1 else next_ref[0]
        left = mended(left, jnp.maximum(tile - 1, 0), slice(W - PAIR, W))
        right = mended(right, jnp.minimum(tile + 1, count - 1), slice(0, PAIR))
        if k == 0:
            left = jnp.where(tile == 0, west_ref[...].astype(F32), left)
        if k == TB - 1:
            right = jnp.where(tile == count - 1, east_ref[...].astype(F32), right)
        left = kept(nb_ref[tile, 2] >= 0, left)
        right = kept(nb_ref[tile, 3] >= 0, right)
        wide = jnp.concatenate([left, mended(field_ref[k], tile, slice(0, W)), right], axis=1)
        taps = with_halo(wide, north_ref[pl.ds(tile, 1), :], south_ref[pl.ds(tile, 1), :])
        store_taps(lhs_ref, k * per, taps)
    for k in range(TB):
        rows = slice(k * per, (k + 1) * per)
        grad = jnp.dot(lhs_ref[rows, :], band_ref[...], preferred_element_type=F32).astype(BF)
        for g in range(GROUPS):
            out_ref[k, :, g * GW : (g + 1) * GW] = grad[g * S : (g + 1) * S]


def field_specs(count, base):
    last = W // PAIR - 1
    return [
        pl.BlockSpec((TB, S, W), lambda i, nb: (i + base, 0, 0)),
        pl.BlockSpec((1, S, PAIR), lambda i, nb: (jnp.maximum((i + base) * TB - 1, 0), 0, last)),
        pl.BlockSpec((1, S, PAIR), lambda i, nb: (jnp.minimum((i + base) * TB + TB, count - 1), 0, 0)),
    ]


def whole(*shape):
    return pl.BlockSpec(shape, lambda i, nb: (0,) * len(shape))


ANY = pl.BlockSpec(memory_space=pl.ANY)
PARAMS = pltpu.CompilerParams(dimension_semantics=("arbitrary",), vmem_limit_bytes=44 * 2**20)
CONSTANTS = ((3 * KW, GW), (4 * CU, GW), (1, GW), (1, GW), (1, GW))
GRADS = ((9, C, C), (C, CU))


def halo_specs(count):
    return [whole(count, PW), whole(count, PW), whole(S, PAIR), whole(S, PAIR)]


def forward(tiles, cotangent, neighbours, constants, base, steps, grads, before=None):
    count = tiles.shape[0]
    rows = TB * GROUPS * S
    more = [] if before is None else [before]
    return pl.pallas_call(
        functools.partial(forward_kernel, base),
        grid_spec=pltpu.PrefetchScalarGridSpec(
            num_scalar_prefetch=1,
            grid=(steps,),
            in_specs=[
                *field_specs(count, base),
                pl.BlockSpec((TB, S, S * CU), lambda i, nb: (i + base, 0, 0)),
                *[whole(*shape) for shape in CONSTANTS + GRADS],
                *[ANY for _ in more],
            ],
            out_specs=[
                pl.BlockSpec((TB, S, W), lambda i, nb: (i + base, 0, 0)),
                whole(4, steps * TB, PW),
                whole(2, steps * TB, S * CU),
                *[whole(*shape) for shape in GRADS],
            ],
            scratch_shapes=[
                pltpu.VMEM((rows, 3 * KW), BF),
                pltpu.VMEM((3 * KW, GW), F32),
                pltpu.VMEM((C, CU), F32),
                pltpu.VMEM((rows, GW), BF),
                pltpu.VMEM((rows, GW), BF),
            ],
        ),
        out_shape=[
            jax.ShapeDtypeStruct((count, S, W), BF),
            jax.ShapeDtypeStruct((4, steps * TB, PW), F32),
            jax.ShapeDtypeStruct((2, steps * TB, S * CU), F32),
            *[jax.ShapeDtypeStruct(shape, F32) for shape in GRADS],
        ],
        input_output_aliases={12: 0} if more else {},
        compiler_params=PARAMS,
        cost_estimate=pl.CostEstimate(flops=steps * 2**32, bytes_accessed=steps * 3 * 2**20, transcendentals=0),
        name=f"forward_{base}",
    )(neighbours, tiles, tiles, tiles, cotangent, *constants, *grads, *more)


def edges(tiles, cotangent, neighbours, kept_rows, halos, constants, grads, delta):
    count = tiles.shape[0]
    ends = count - 1
    (rows_a, cot_a), (rows_b, cot_b) = kept_rows
    own = (count, W)
    sent = (count, W + PAIR)
    return pl.pallas_call(
        edge_kernel,
        grid_spec=pltpu.PrefetchScalarGridSpec(
            num_scalar_prefetch=1,
            grid=(4,),
            in_specs=[
                pl.BlockSpec((1, S, W), lambda i, nb: (ends * jnp.minimum(i, 1), 0, 0)),
                pl.BlockSpec((1, S, PAIR), lambda i, nb: (ends - 1, 0, W // PAIR - 1)),
                pl.BlockSpec((1, S, PAIR), lambda i, nb: (1, 0, 0)),
                pl.BlockSpec((1, S, S * CU), lambda i, nb: (ends * jnp.minimum(i, 1), 0, 0)),
                *[whole(*value.shape) for value in (rows_a, rows_b, cot_a, cot_b)],
                *halo_specs(count),
                *[whole(*shape) for shape in CONSTANTS + GRADS],
                ANY,
            ],
            out_specs=[
                pl.BlockSpec((1, S, W), lambda i, nb: (ends * jnp.minimum(i, 1), 0, 0)),
                whole(*sent), whole(*sent), whole(*own), whole(*own),
                *[whole(*shape) for shape in GRADS],
            ],
            scratch_shapes=[
                pltpu.VMEM((GROUPS * S, 3 * KW), BF),
                pltpu.VMEM((GROUPS * S, 4 * CU), BF),
                pltpu.VMEM((3 * KW, GW), F32),
                pltpu.VMEM((C, CU), F32),
            ],
        ),
        out_shape=[
            jax.ShapeDtypeStruct((count, S, W), BF),
            jax.ShapeDtypeStruct(sent, BF),
            jax.ShapeDtypeStruct(sent, BF),
            jax.ShapeDtypeStruct(own, F32),
            jax.ShapeDtypeStruct(own, F32),
            *[jax.ShapeDtypeStruct(shape, F32) for shape in GRADS],
        ],
        input_output_aliases={20: 0},
        compiler_params=PARAMS,
        cost_estimate=pl.CostEstimate(flops=2**33, bytes_accessed=2**22, transcendentals=0),
        name="edges",
    )(neighbours, tiles, tiles, tiles, cotangent, rows_a, rows_b, cot_a, cot_b, *halos, *constants, *grads, delta)


def backward(delta, halos, own, neighbours, bands, base, steps, before=None):
    count = delta.shape[0]
    rows = TB * GROUPS * S
    more = [] if before is None else [before]
    return pl.pallas_call(
        functools.partial(backward_kernel, base),
        grid_spec=pltpu.PrefetchScalarGridSpec(
            num_scalar_prefetch=1,
            grid=(steps,),
            in_specs=[
                *field_specs(count, base), *halo_specs(count), whole(count, W), whole(count, W), whole(3 * KW, GW),
                *[ANY for _ in more],
            ],
            out_specs=pl.BlockSpec((TB, S, W), lambda i, nb: (i + base, 0, 0)),
            scratch_shapes=[pltpu.VMEM((rows, 3 * KW), BF)],
        ),
        out_shape=jax.ShapeDtypeStruct((count, S, W), BF),
        input_output_aliases={11: 0} if more else {},
        compiler_params=PARAMS,
        cost_estimate=pl.CostEstimate(flops=steps * 2**31, bytes_accessed=steps * 2**20, transcendentals=0),
        name=f"backward_{base}",
    )(neighbours, delta, delta, delta, *halos, *own, bands, *more)


def swapped(value, move):
    cells = [(x, z, y, c) for x in range(4) for z in range(4) for y in range(4) for c in range(2)]
    number = {cell: i for i, cell in enumerate(cells)}
    return lax.ppermute(value, AXES, [(number[cell], number[move(cell)]) for cell in cells])


def flip(axis, second):
    def move(cell):
        there = list(cell)
        there[axis] = 3 - cell[axis] if second else cell[axis] ^ 1
        return tuple(there)

    return move


def tied(*values):
    return lax.optimization_barrier(values)


def local(tiles, cotangent, neighbours, conv_weight, expand_weight, norm_scale, norm_shift):
    count = tiles.shape[0]
    position = lax.axis_index("space")
    kernel = conv_weight.reshape(3, 3, C, C)
    flipped = jnp.transpose(jnp.flip(kernel, (0, 1)), (0, 1, 3, 2))
    turned = expand_weight.T
    wide = jnp.concatenate([jnp.pad(turned, ((CU * j, CU * (3 - j)), (0, 0))) for j in range(4)], axis=1)
    scale = jnp.tile(norm_scale, 4)[None]
    half_shift = 0.5 * jnp.tile(norm_shift, 4)[None]
    constants = (band(kernel), wide, 0.5 * scale, half_shift, scale)
    down = jnp.concatenate([tiles[:, S - 1], tiles[count - 1, :, W - PAIR :]], axis=1)
    up = jnp.concatenate([tiles[:, 0], tiles[0, :, :PAIR]], axis=1)
    blocks = count // TB
    early = blocks // 2

    near = halo_near(down, up)
    grads = tuple(jnp.zeros(shape, F32) for shape in GRADS)
    delta, *first_rows, conv_part, expand_part = forward(tiles, cotangent, neighbours, constants, 0, early, grads)
    near, delta = tied(near, delta)
    far = halo_far(down, up, near)
    delta, *last_rows, conv_part, expand_part = forward(
        tiles, cotangent, neighbours, constants, early, blocks - early, (conv_part, expand_part), delta
    )
    far, delta = tied(far, delta)
    halos = halo(down, up, near, far, neighbours, position)
    delta, up, down, top, bottom, conv_part, expand_part = edges(
        tiles, cotangent, neighbours, (first_rows, last_rows), halos, constants, (conv_part, expand_part), delta
    )

    part = jnp.concatenate([conv_part.reshape(9 * 32, 2 * C), expand_part.reshape(2 * C, 2 * C)], axis=0)
    half = part.shape[0] // 2
    even = lax.axis_index("space") % 2 == 0
    low, high = part[:half], part[half:]
    near = halo_near(down, up)
    other = swapped(jnp.where(even, high, low), flip(3, False))
    near, other = tied(near, other)
    part = jnp.where(even, low, high) + other
    far = halo_far(down, up, near)
    back = band(flipped)
    grad = None
    counts = [blocks * (i + 1) // PIECES - blocks * i // PIECES for i in range(PIECES)]
    halos = None
    for turn in range(6):
        other = swapped(part, flip(turn // 2, turn % 2 == 1))
        piece = turn - (6 - PIECES)
        if piece >= 0:
            if halos is None:
                halos = halo(down, up, near, far, neighbours, position)
            grad = backward(delta, halos, (top, bottom), neighbours, back, sum(counts[:piece]), counts[piece], grad)
            other, grad = tied(other, grad)
        part = part + other
        if grad is not None:
            part, grad = tied(part, grad)
        elif turn == 5 - PIECES:
            part, far = tied(part, far)
    other = swapped(part, flip(3, False))
    total = jnp.concatenate([jnp.where(even, part, other), jnp.where(even, other, part)], axis=0)
    cells = lax.axis_size("dp") * lax.axis_size("space") * count * S * S
    total = total * (1.0 / math.sqrt(cells))
    return grad, total[: 9 * 32].reshape(9, C * C), total[9 * 32 :].reshape(C, CU)


def solution(mesh):
    placed = (P(AXES, None, None), P(AXES, None, None), P(AXES, None), P(), P(), P(), P())
    return jax.shard_map(
        local,
        mesh=mesh,
        in_specs=placed,
        out_specs=(P(AXES, None, None), P(), P()),
        check_vma=False,
    )
```

time: 141 us -> 121 us (0.86)
  waiting for transfers between devices: 23.2 us -> 6.9 us
  starting transfers between devices: 61.7 us -> 45.6 us
  Pallas kernels: 40.1 us -> 55.7 us
  local copies, waits for them, and re-layouts: 10.6 us -> 7.5 us
    pallas_call x2 -> x7, Pallas kernels: 40.1 us -> 55.7 us  [the longest x2 32.6 us: forward(): pl.pallas_call(functools.partial(forward_kernel, base), grid_spec=pltpu.P...]
    ppermute x12 -> x8, starting transfers between devices: 38.4 us -> 23.7 us  [shifted(): return lax.ppermute(value, 'space', pairs)]
    ppermute x8, waiting for transfers between devices: 16.4 us -> 4.91 us  [swapped(): lax.ppermute(value, AXES, [(number[cell], number[move(cell)]) for cell in...]
    ppermute x12 -> x8, waiting for transfers between devices: 6.83 us -> 1.99 us  [shifted(): return lax.ppermute(value, 'space', pairs)]
    pallas_call x1 -> x0, local copies, waits for them, and re-layouts: 4.49 us -> none  [forward(): pl.pallas_call(forward_kernel, grid_spec=pltpu.PrefetchScalarGridSpec(num...]
    unnamed x16 -> x22, local copies, waits for them, and re-layouts: 0.38 us -> 2.45 us
  transfers between devices with their start and end apart: 20 -> 16, of which waited for: 10 -> 4; matrix products, arithmetic and copies ran while one was open for 3% -> 2% of each run, Pallas kernels for 7% -> 39%
where the time goes in v2:
time: 121 us
  Pallas kernels  55.7 us (46%)
  starting transfers between devices  45.6 us (38%)
  local copies, waits for them, and re-layouts  7.5 us (6%)
  waiting for transfers between devices  6.9 us (6%)
  matrix products  2.48 us (2%)
    pallas_call x2, Pallas kernels, forward(): pl.pallas_call(functools.partial(forward_kernel, base), grid_spec=pltpu.P...  32.6 us
    ppermute x8, starting transfers between devices, shifted(): return lax.ppermute(value, 'space', pairs)  23.7 us
    ppermute x8, starting transfers between devices, swapped(): lax.ppermute(value, AXES, [(number[cell], number[move(cell)]) for cell in...  21.9 us
    pallas_call x4, Pallas kernels, backward(): pl.pallas_call(functools.partial(backward_kernel, base), grid_spec=pltpu....  14.8 us
    pallas_call x1, Pallas kernels, edges(): pl.pallas_call(edge_kernel, grid_spec=pltpu.PrefetchScalarGridSpec(num_sc...  8.29 us
    ppermute x8, waiting for transfers between devices, swapped(): lax.ppermute(value, AXES, [(number[cell], number[move(cell)]) for cell in...  4.91 us
    dot_general x12, matrix products, pick(): return jnp.dot(chosen, window[:, lanes], preferred_element_type=F32)  2.48 us
    unnamed x22, local copies, waits for them, and re-layouts  2.45 us
  transfers between devices with their start and end apart: 16, of which 4 were waited for; matrix products, arithmetic and copies ran while one was open for 2% of the time, Pallas kernels for 39%

profile of v2, /device:TPU:1, one launch (start us, length us, event | category | flops | bytes accessed | tf_op | source)
XLA Modules:
  0.0 120.5 jit_solution(7951076971792531578)
XLA Ops:
  0.7 2.0 %fusion.101 = (bf16[32,1,2048]{2,1,0:T(2,128)(2,1)S(1)}, bf16[32,1,2048]{2,1,0:T(2,128)(2,1)S(1)}) fusion(bf16[32,32,2048]{2,1,0:T(8,128)(2,1)} %next_ref.5), kind=kLoop, calls=%fused_computation.174 | loop fusion | bytes 524288 | tf_op jit(solution)/shard_map/slice | solution.py:490
  2.7 0.7 slice_bitcast_fusion
  3.5 4.6 %collective-permute-start = (bf16[32,2176]{1,0:T(8,128)(2,1)S(1)}, bf16[32,2176]{1,0:T(8,128)(2,1)S(1)}, u32[]{:S(2)}, u32[]{:S(2)}) collective-permute-start(bf16[32,2176]{1,0:T(8,128)(2,1)S(1)} %pad_maximum_fusion.10), channel_id=1, source_target_pairs={{0,1},{1,2},{2,3},{3,4},{4,5},{5,6},{6,7},{7,8},{8,9},{9,10},{10,1... | collective-permute-start | bytes 417800 | tf_op jit(solution)/shard_map/ppermute | solution.py:31
  8.2 1.9 %collective-permute-start.1 = (bf16[32,2176]{1,0:T(8,128)(2,1)S(1)}, bf16[32,2176]{1,0:T(8,128)(2,1)S(1)}, u32[]{:S(2)}, u32[]{:S(2)}) collective-permute-start(bf16[32,2176]{1,0:T(8,128)(2,1)S(1)} %pad_maximum_fusion.11), channel_id=1, source_target_pairs={{1,0},{2,1},{3,2},{4,3},{5,4},{6,5},{7,6},{8,7},{9,8},{10,9},{11,1... | collective-permute-start | bytes 417800 | tf_op jit(solution)/shard_map/ppermute | solution.py:31
  11.6 16.2 %forward_0.1 = (bf16[32,32,2048]{2,1,0:T(8,128)(2,1)S(1)}, f32[4,16,2304]{2,1,0:T(8,128)S(1)}, f32[2,16,8192]{2,1,0:T(8,128)S(1)}, f32[9,64,64]{2,1,0:T(8,128)S(1)}, f32[64,256]{1,0:T(8,128)S(1)}) custom-call(s32[32,8]{1,0:T(8,128)S(1)} %copy.31.nb_ref, bf16[32,32,2048]{2,1,0:T(8,128)(2,1)} %next_ref.5, bf16[32,32,2048]{2,1,0:T(8,128)(2,1)} %next_ref.5, ...), custom_call_target="tpu_custom_call" | custom-call | flops 17179869184 | bytes 12582912 | tf_op jit(solution)/shard_map/forward_0/pallas_call | solution.py:350
  28.1 3.2 %collective-permute-start.2 = (bf16[64,2176]{1,0:T(8,128)(2,1)S(1)}, bf16[64,2176]{1,0:T(8,128)(2,1)S(1)}, u32[]{:S(2)}, u32[]{:S(2)}) collective-permute-start(bf16[64,2176]{1,0:T(8,128)(2,1)S(1)} %pad_maximum_fusion.6), channel_id=1, source_target_pairs={{0,2},{1,3},{2,4},{3,5},{4,6},{5,7},{6,8},{7,9},{8,10},{9,11},{10,... | collective-permute-start | bytes 835592 | tf_op jit(solution)/shard_map/ppermute | solution.py:31
  31.3 1.3 %collective-permute-start.3 = (bf16[64,2176]{1,0:T(8,128)(2,1)S(1)}, bf16[64,2176]{1,0:T(8,128)(2,1)S(1)}, u32[]{:S(2)}, u32[]{:S(2)}) collective-permute-start(bf16[64,2176]{1,0:T(8,128)(2,1)S(1)} %pad_maximum_fusion.7), channel_id=1, source_target_pairs={{2,0},{3,1},{4,2},{5,3},{6,4},{7,5},{8,6},{9,7},{10,8},{11,9},{12,... | collective-permute-start | bytes 835592 | tf_op jit(solution)/shard_map/ppermute | solution.py:31
  32.6 16.4 %forward_4.1 = (bf16[32,32,2048]{2,1,0:T(8,128)(2,1)S(1)}, f32[4,16,2304]{2,1,0:T(8,128)S(1)}, f32[2,16,8192]{2,1,0:T(8,128)S(1)}, f32[9,64,64]{2,1,0:T(8,128)S(1)}, f32[64,256]{1,0:T(8,128)S(1)}) custom-call(s32[32,8]{1,0:T(8,128)S(1)} %copy.31.nb_ref, bf16[32,32,2048]{2,1,0:T(8,128)(2,1)} %next_ref.5, ...), custom_call_target="tpu_custom_call", output_to_operand_aliasing={{0}: (12, {})} | custom-call | flops 17179869184 | bytes 12582912 | tf_op jit(solution)/shard_map/forward_4/pallas_call | solution.py:350
  49.1 2.0 %copy-done = bf16[32,32,2048]{2,1,0:T(8,128)(2,1)} copy-done((bf16[32,32,2048]{2,1,0:T(8,128)(2,1)}, bf16[32,32,2048]{2,1,0:T(8,128)(2,1)S(1)}, u32[]{:S(2)}) %copy-start) | copy-done | bytes 4194328
  52.0 0.3 fusion.29
  52.2 0.3 fusion.31
  52.5 8.3 %edges.1 = (bf16[32,32,2048]{2,1,0:T(8,128)(2,1)}, bf16[32,2176]{1,0:T(8,128)(2,1)S(1)}, bf16[32,2176]{1,0:T(8,128)(2,1)S(1)}, f32[32,2048]{1,0:T(8,128)S(1)}, f...) custom-call(s32[32,8]{1,0:T(8,128)S(1)} %copy.31.nb_ref, ...), custom_call_target="tpu_custom_call", output_to_operand_aliasing={{0}: (20, {})} | custom-call | flops 8589934592 | bytes 4194304 | tf_op jit(solution)/shard_map/edges/pallas_call | solution.py:394
  60.8 2.7 %collective-permute-start.5 = (bf16[32,2176]{1,0:T(8,128)(2,1)S(1)}, bf16[32,2176]{1,0:T(8,128)(2,1)S(1)}, u32[]{:S(2)}, u32[]{:S(2)}) collective-permute-start(bf16[32,2176]{1,0:T(8,128)(2,1)S(1)} %get-tuple-element.67), channel_id=1, source_target_pairs={{1,0},{2,1},{3,2},{4,3},{5,4},{6,5},{7,6},{8,7},{9,8},{10,9},{11,1... | collective-permute-start | bytes 417800 | tf_op jit(solution)/shard_map/ppermute | solution.py:31
  63.8 4.6 %collective-permute-start.4 = (bf16[32,2176]{1,0:T(8,128)(2,1)S(1)}, bf16[32,2176]{1,0:T(8,128)(2,1)S(1)}, u32[]{:S(2)}, u32[]{:S(2)}) collective-permute-start(bf16[32,2176]{1,0:T(8,128)(2,1)S(1)} %get-tuple-element.66), channel_id=1, source_target_pairs={{0,1},{1,2},{2,3},{3,4},{4,5},{5,6},{6,7},{7,8},{8,9},{9,10},{10,1... | collective-permute-start | bytes 417800 | tf_op jit(solution)/shard_map/ppermute | solution.py:31
  68.5 2.0 %collective-permute-done.4 = bf16[32,2176]{1,0:T(8,128)(2,1)S(1)} collective-permute-done((bf16[32,2176]{1,0:T(8,128)(2,1)S(1)}, bf16[32,2176]{1,0:T(8,128)(2,1)S(1)}, u32[]{:S(2)}, u32[]{:S(2)}) %collective-permute-start.4) | collective-permute-done | bytes 139296 | tf_op jit(solution)/shard_map/ppermute | solution.py:31
  70.5 1.5 %collective-permute-start.10 = (bf16[64,2176]{1,0:T(8,128)(2,1)S(1)}, bf16[64,2176]{1,0:T(8,128)(2,1)S(1)}, u32[]{:S(2)}, u32[]{:S(2)}) collective-permute-start(bf16[64,2176]{1,0:T(8,128)(2,1)S(1)} %pad_maximum_fusion.9), channel_id=1, source_target_pairs={{2,0},{3,1},{4,2},{5,3},{6,4},{7,5},{8,6},{9,7},{10,8},{11,9},{12,... | collective-permute-start | bytes 835592 | tf_op jit(solution)/shard_map/ppermute | solution.py:31
  72.0 1.3 %collective-permute-start.7 = (f32[208,128]{1,0:T(8,128)S(1)}, f32[208,128]{1,0:T(8,128)S(1)}, u32[]{:S(2)}, u32[]{:S(2)}) collective-permute-start(f32[208,128]{1,0:T(8,128)S(1)} %select_add_fusion), channel_id=1, source_target_pairs={{0,32},{1,33},{2,34},{3,35},{4,36},{5,37},{6,38},{7,39},{8,40},{9,... | collective-permute-start | bytes 319496 | tf_op jit(solution)/shard_map/ppermute | solution.py:463
  73.3 3.8 %collective-permute-start.9 = (bf16[64,2176]{1,0:T(8,128)(2,1)S(1)}, bf16[64,2176]{1,0:T(8,128)(2,1)S(1)}, u32[]{:S(2)}, u32[]{:S(2)}) collective-permute-start(bf16[64,2176]{1,0:T(8,128)(2,1)S(1)} %pad_maximum_fusion.8), channel_id=1, source_target_pairs={{0,2},{1,3},{2,4},{3,5},{4,6},{5,7},{6,8},{7,9},{8,10},{9,11},{10,... | collective-permute-start | bytes 835592 | tf_op jit(solution)/shard_map/ppermute | solution.py:31
  77.2 1.9 %collective-permute-start.8 = (f32[208,128]{1,0:T(8,128)S(1)}, f32[208,128]{1,0:T(8,128)S(1)}, u32[]{:S(2)}, u32[]{:S(2)}) collective-permute-start(f32[208,128]{1,0:T(8,128)S(1)} %add.149), channel_id=1, source_target_pairs={{0,96},{1,97},{2,98},{3,99},{4,100},{5,101},{6,102},{7,103},{8,104... | collective-permute-start | bytes 319496 | tf_op jit(solution)/shard_map/ppermute | solution.py:463
  79.2 2.9 %collective-permute-done.8 = f32[208,128]{1,0:T(8,128)S(1)} collective-permute-done((f32[208,128]{1,0:T(8,128)S(1)}, f32[208,128]{1,0:T(8,128)S(1)}, u32[]{:S(2)}, u32[]{:S(2)}) %collective-permute-start.8) | collective-permute-done | bytes 106528 | tf_op jit(solution)/shard_map/ppermute | solution.py:463
  82.8 0.2 fusion.27
  83.4 10.4 %collective-permute-start.11 = (f32[208,128]{1,0:T(8,128)S(1)}, f32[208,128]{1,0:T(8,128)S(1)}, u32[]{:S(2)}, u32[]{:S(2)}) collective-permute-start(f32[208,128]{1,0:T(8,128)S(1)} %add.150), channel_id=1, source_target_pairs={{0,8},{1,9},{2,10},{3,11},{4,12},{5,13},{6,14},{7,15},{8,0},{9,1},... | collective-permute-start | bytes 319496 | tf_op jit(solution)/shard_map/ppermute | solution.py:463
  93.9 3.7 %backward_0.1.rest_0_ = bf16[32,32,2048]{2,1,0:T(8,128)(2,1)} custom-call(s32[32,8]{1,0:T(8,128)S(1)} %copy.31.nb_ref, bf16[32,32,2048]{2,1,0:T(8,128)(2,1)S(1)} %copy-done.1, bf16[32,32,2048]{2,1,0:T(8,128)(2,1)S(1)} %copy-done.1, bf16[32,32,2048]{2,1,0:T(8,128)(2,1)S(1)} %copy-done.1, f32[32,2304]{1,0:T(8,128)S(1)} %pad_maximum_fusion.4.north_ref, ...), custom_call_target="tpu_custom_call" | custom-call | flops 4294967296 | bytes 2097152 | tf_op jit(solution)/shard_map/backward_0/pallas_call | solution.py:440
  97.6 2.3 %collective-permute-start.12 = (f32[208,128]{1,0:T(8,128)S(1)}, f32[208,128]{1,0:T(8,128)S(1)}, u32[]{:S(2)}, u32[]{:S(2)}) collective-permute-start(f32[208,128]{1,0:T(8,128)S(1)} %add.151), channel_id=1, source_target_pairs={{0,24},{1,25},{2,26},{3,27},{4,28},{5,29},{6,30},{7,31},{8,16},{9,... | collective-permute-start | bytes 319496 | tf_op jit(solution)/shard_map/ppermute | solution.py:463
  99.9 3.7 %backward_2.1.rest_0_ = bf16[32,32,2048]{2,1,0:T(8,128)(2,1)} custom-call(s32[32,8]{1,0:T(8,128)S(1)} %copy.31.nb_ref, bf16[32,32,2048]{2,1,0:T(8,128)(2,1)S(1)} %copy-done.1, bf16[32,32,2048]{2,1,0:T(8,128)(2,1)S(1)} %copy-done.1, bf16[32,32,2048]{2,1,0:T(8,128)(2,1)S(1)} %copy-done.1, ...), custom_call_target="tpu_custom_call", output_to_operand_aliasing={{}: (11, {})} | custom-call | flops 4294967296 | bytes 2097152 | tf_op jit(solution)/shard_map/backward_2/pallas_call | solution.py:440
  103.7 3.7 %backward_4.1.rest_0_ = bf16[32,32,2048]{2,1,0:T(8,128)(2,1)} custom-call(s32[32,8]{1,0:T(8,128)S(1)} %copy.31.nb_ref, bf16[32,32,2048]{2,1,0:T(8,128)(2,1)S(1)} %copy-done.1, bf16[32,32,2048]{2,1,0:T(8,128)(2,1)S(1)} %copy-done.1, bf16[32,32,2048]{2,1,0:T(8,128)(2,1)S(1)} %copy-done.1, ...), custom_call_target="tpu_custom_call", output_to_operand_aliasing={{}: (11, {})} | custom-call | flops 4294967296 | bytes 2097152 | tf_op jit(solution)/shard_map/backward_4/pallas_call | solution.py:440
  107.6 3.7 %backward_6.1 = bf16[32,32,2048]{2,1,0:T(8,128)(2,1)} custom-call(s32[32,8]{1,0:T(8,128)S(1)} %copy.31.nb_ref, bf16[32,32,2048]{2,1,0:T(8,128)(2,1)S(1)} %copy-done.1, bf16[32,32,2048]{2,1,0:T(8,128)(2,1)S(1)} %copy-done.1, bf16[32,32,2048]{2,1,0:T(8,128)(2,1)S(1)} %copy-done.1, ...), custom_call_target="tpu_custom_call", output_to_operand_aliasing={{}: (11, {})} | custom-call | flops 4294967296 | bytes 2097152 | tf_op jit(solution)/shard_map/backward_6/pallas_call | solution.py:440
  111.3 1.0 collective-permute-done.14
  112.3 5.8 %collective-permute-start.15 = (f32[208,128]{1,0:T(8,128)S(1)}, f32[208,128]{1,0:T(8,128)S(1)}, u32[]{:S(2)}, u32[]{:S(2)}) collective-permute-start(f32[208,128]{1,0:T(8,128)S(1)} %add.154), channel_id=1, source_target_pairs={{0,1},{1,0},{2,3},{3,2},{4,5},{5,4},{6,7},{7,6},{8,9},{9,8},{10,11... | collective-permute-start | bytes 319496 | tf_op jit(solution)/shard_map/ppermute | solution.py:463
  118.1 1.0 collective-permute-done.15
  119.2 0.7 reshape.64
  119.9 0.6 reshape.65
  (92 shorter events, 4.5 us)
Async XLA Ops:
  0.6 9.5 %copy-start.4 = (s32[32,8]{0,1:T(8,128)S(1)}, s32[32,8]{0,1:T(8,128)}, u32[]{:S(2)}) copy-start(s32[32,8]{0,1:T(8,128)} %param.9) | copy-start | bytes 3076
  0.6 9.7 %copy-start.2 = (bf16[9,4096]{1,0:T(8,128)(2,1)S(1)}, bf16[9,4096]{1,0:T(8,128)(2,1)}, u32[]{:S(2)}) copy-start(bf16[9,4096]{1,0:T(8,128)(2,1)} %param.10) | copy-start | bytes 221188
  0.7 10.1 %copy-start.5 = (f32[64]{0:T(128)S(1)}, f32[64]{0:T(128)}, u32[]{:S(2)}) copy-start(f32[64]{0:T(128)} %param.12) | copy-start | bytes 772
  2.7 8.4 %copy-start.3 = (bf16[64,256]{1,0:T(8,128)(2,1)S(1)}, bf16[64,256]{1,0:T(8,128)(2,1)}, u32[]{:S(2)}) copy-start(bf16[64,256]{1,0:T(8,128)(2,1)} %param.11) | copy-start | bytes 98308
  3.5 7.8 %copy-start.6 = (f32[64]{0:T(128)S(1)}, f32[64]{0:T(128)}, u32[]{:S(2)}) copy-start(f32[64]{0:T(128)} %param.13) | copy-start | bytes 772
  3.5 24.5 %collective-permute-start = (bf16[32,2176]{1,0:T(8,128)(2,1)S(1)}, bf16[32,2176]{1,0:T(8,128)(2,1)S(1)}, u32[]{:S(2)}, u32[]{:S(2)}) collective-permute-start(bf16[32,2176]{1,0:T(8,128)(2,1)S(1)} %pad_maximum_fusion.10), channel_id=1, source_target_pairs={{0,1},{1,2},{2,3},{3,4},{4,5},{5,6},{6,7},{7,8},{8,9},{9,10},{10,1... | collective-permute-start | bytes 417800 | tf_op jit(solution)/shard_map/ppermute | solution.py:31
  8.2 19.8 %collective-permute-start.1 = (bf16[32,2176]{1,0:T(8,128)(2,1)S(1)}, bf16[32,2176]{1,0:T(8,128)(2,1)S(1)}, u32[]{:S(2)}, u32[]{:S(2)}) collective-permute-start(bf16[32,2176]{1,0:T(8,128)(2,1)S(1)} %pad_maximum_fusion.11), channel_id=1, source_target_pairs={{1,0},{2,1},{3,2},{4,3},{5,4},{6,5},{7,6},{8,7},{9,8},{10,9},{11,1... | collective-permute-start | bytes 417800 | tf_op jit(solution)/shard_map/ppermute | solution.py:31
  28.1 23.0 %collective-permute-start.2 = (bf16[64,2176]{1,0:T(8,128)(2,1)S(1)}, bf16[64,2176]{1,0:T(8,128)(2,1)S(1)}, u32[]{:S(2)}, u32[]{:S(2)}) collective-permute-start(bf16[64,2176]{1,0:T(8,128)(2,1)S(1)} %pad_maximum_fusion.6), channel_id=1, source_target_pairs={{0,2},{1,3},{2,4},{3,5},{4,6},{5,7},{6,8},{7,9},{8,10},{9,11},{10,... | collective-permute-start | bytes 835592 | tf_op jit(solution)/shard_map/ppermute | solution.py:31
  31.3 19.8 %collective-permute-start.3 = (bf16[64,2176]{1,0:T(8,128)(2,1)S(1)}, bf16[64,2176]{1,0:T(8,128)(2,1)S(1)}, u32[]{:S(2)}, u32[]{:S(2)}) collective-permute-start(bf16[64,2176]{1,0:T(8,128)(2,1)S(1)} %pad_maximum_fusion.7), channel_id=1, source_target_pairs={{2,0},{3,1},{4,2},{5,3},{6,4},{7,5},{8,6},{9,7},{10,8},{11,9},{12,... | collective-permute-start | bytes 835592 | tf_op jit(solution)/shard_map/ppermute | solution.py:31
  49.1 2.0 %copy-start = (bf16[32,32,2048]{2,1,0:T(8,128)(2,1)}, bf16[32,32,2048]{2,1,0:T(8,128)(2,1)S(1)}, u32[]{:S(2)}) copy-start(bf16[32,32,2048]{2,1,0:T(8,128)(2,1)S(1)} %get-tuple-element.63.delta_in_ref) | copy-start | bytes 12582916
  60.8 9.6 %collective-permute-start.5 = (bf16[32,2176]{1,0:T(8,128)(2,1)S(1)}, bf16[32,2176]{1,0:T(8,128)(2,1)S(1)}, u32[]{:S(2)}, u32[]{:S(2)}) collective-permute-start(bf16[32,2176]{1,0:T(8,128)(2,1)S(1)} %get-tuple-element.67), channel_id=1, source_target_pairs={{1,0},{2,1},{3,2},{4,3},{5,4},{6,5},{7,6},{8,7},{9,8},{10,9},{11,1... | collective-permute-start | bytes 417800 | tf_op jit(solution)/shard_map/ppermute | solution.py:31
  63.7 4.8 %collective-permute-start.6 = (f32[208,128]{1,0:T(8,128)S(1)}, f32[208,128]{1,0:T(8,128)S(1)}, u32[]{:S(2)}, u32[]{:S(2)}) collective-permute-start(f32[208,128]{1,0:T(8,128)S(1)} %slice_select_fusion), channel_id=1, source_target_pairs={{0,1},{1,0},{2,3},{3,2},{4,5},{5,4},{6,7},{7,6},{8,9},{9,8},{10,11... | collective-permute-start | bytes 319496 | tf_op jit(solution)/shard_map/ppermute | solution.py:463
  63.8 6.6 %collective-permute-start.4 = (bf16[32,2176]{1,0:T(8,128)(2,1)S(1)}, bf16[32,2176]{1,0:T(8,128)(2,1)S(1)}, u32[]{:S(2)}, u32[]{:S(2)}) collective-permute-start(bf16[32,2176]{1,0:T(8,128)(2,1)S(1)} %get-tuple-element.66), channel_id=1, source_target_pairs={{0,1},{1,2},{2,3},{3,4},{4,5},{5,6},{6,7},{7,8},{8,9},{9,10},{10,1... | collective-permute-start | bytes 417800 | tf_op jit(solution)/shard_map/ppermute | solution.py:31
  70.5 11.6 %collective-permute-start.10 = (bf16[64,2176]{1,0:T(8,128)(2,1)S(1)}, bf16[64,2176]{1,0:T(8,128)(2,1)S(1)}, u32[]{:S(2)}, u32[]{:S(2)}) collective-permute-start(bf16[64,2176]{1,0:T(8,128)(2,1)S(1)} %pad_maximum_fusion.9), channel_id=1, source_target_pairs={{2,0},{3,1},{4,2},{5,3},{6,4},{7,5},{8,6},{9,7},{10,8},{11,9},{12,... | collective-permute-start | bytes 835592 | tf_op jit(solution)/shard_map/ppermute | solution.py:31
  72.0 5.2 %collective-permute-start.7 = (f32[208,128]{1,0:T(8,128)S(1)}, f32[208,128]{1,0:T(8,128)S(1)}, u32[]{:S(2)}, u32[]{:S(2)}) collective-permute-start(f32[208,128]{1,0:T(8,128)S(1)} %select_add_fusion), channel_id=1, source_target_pairs={{0,32},{1,33},{2,34},{3,35},{4,36},{5,37},{6,38},{7,39},{8,40},{9,... | collective-permute-start | bytes 319496 | tf_op jit(solution)/shard_map/ppermute | solution.py:463
  73.3 8.8 %collective-permute-start.9 = (bf16[64,2176]{1,0:T(8,128)(2,1)S(1)}, bf16[64,2176]{1,0:T(8,128)(2,1)S(1)}, u32[]{:S(2)}, u32[]{:S(2)}) collective-permute-start(bf16[64,2176]{1,0:T(8,128)(2,1)S(1)} %pad_maximum_fusion.8), channel_id=1, source_target_pairs={{0,2},{1,3},{2,4},{3,5},{4,6},{5,7},{6,8},{7,9},{8,10},{9,11},{10,... | collective-permute-start | bytes 835592 | tf_op jit(solution)/shard_map/ppermute | solution.py:31
  77.2 4.8 %collective-permute-start.8 = (f32[208,128]{1,0:T(8,128)S(1)}, f32[208,128]{1,0:T(8,128)S(1)}, u32[]{:S(2)}, u32[]{:S(2)}) collective-permute-start(f32[208,128]{1,0:T(8,128)S(1)} %add.149), channel_id=1, source_target_pairs={{0,96},{1,97},{2,98},{3,99},{4,100},{5,101},{6,102},{7,103},{8,104... | collective-permute-start | bytes 319496 | tf_op jit(solution)/shard_map/ppermute | solution.py:463
  82.1 11.8 %copy-start.1 = (bf16[32,32,2048]{2,1,0:T(8,128)(2,1)S(1)}, bf16[32,32,2048]{2,1,0:T(8,128)(2,1)}, u32[]{:S(2)}) copy-start(bf16[32,32,2048]{2,1,0:T(8,128)(2,1)} %get-tuple-element.72.field_ref.prev_ref.next_ref) | copy-start | bytes 12582916
  83.4 14.1 %collective-permute-start.11 = (f32[208,128]{1,0:T(8,128)S(1)}, f32[208,128]{1,0:T(8,128)S(1)}, u32[]{:S(2)}, u32[]{:S(2)}) collective-permute-start(f32[208,128]{1,0:T(8,128)S(1)} %add.150), channel_id=1, source_target_pairs={{0,8},{1,9},{2,10},{3,11},{4,12},{5,13},{6,14},{7,15},{8,0},{9,1},... | collective-permute-start | bytes 319496 | tf_op jit(solution)/shard_map/ppermute | solution.py:463
  97.6 6.0 %collective-permute-start.12 = (f32[208,128]{1,0:T(8,128)S(1)}, f32[208,128]{1,0:T(8,128)S(1)}, u32[]{:S(2)}, u32[]{:S(2)}) collective-permute-start(f32[208,128]{1,0:T(8,128)S(1)} %add.151), channel_id=1, source_target_pairs={{0,24},{1,25},{2,26},{3,27},{4,28},{5,29},{6,30},{7,31},{8,16},{9,... | collective-permute-start | bytes 319496 | tf_op jit(solution)/shard_map/ppermute | solution.py:463
  103.6 3.8 %collective-permute-start.13 = (f32[208,128]{1,0:T(8,128)S(1)}, f32[208,128]{1,0:T(8,128)S(1)}, u32[]{:S(2)}, u32[]{:S(2)}) collective-permute-start(f32[208,128]{1,0:T(8,128)S(1)} %add.152), channel_id=1, source_target_pairs={{0,2},{1,3},{2,0},{3,1},{4,6},{5,7},{6,4},{7,5},{8,10},{9,11},{10,... | collective-permute-start | bytes 319496 | tf_op jit(solution)/shard_map/ppermute | solution.py:463
  107.5 4.8 %collective-permute-start.14 = (f32[208,128]{1,0:T(8,128)S(1)}, f32[208,128]{1,0:T(8,128)S(1)}, u32[]{:S(2)}, u32[]{:S(2)}) collective-permute-start(f32[208,128]{1,0:T(8,128)S(1)} %add.153), channel_id=1, source_target_pairs={{0,6},{1,7},{2,4},{3,5},{4,2},{5,3},{6,0},{7,1},{8,14},{9,15},{10,... | collective-permute-start | bytes 319496 | tf_op jit(solution)/shard_map/ppermute | solution.py:463
  112.3 6.7 %collective-permute-start.15 = (f32[208,128]{1,0:T(8,128)S(1)}, f32[208,128]{1,0:T(8,128)S(1)}, u32[]{:S(2)}, u32[]{:S(2)}) collective-permute-start(f32[208,128]{1,0:T(8,128)S(1)} %add.154), channel_id=1, source_target_pairs={{0,1},{1,0},{2,3},{3,2},{4,5},{5,4},{6,7},{7,6},{8,9},{9,8},{10,11... | collective-permute-start | bytes 319496 | tf_op jit(solution)/shard_map/ppermute | solution.py:463

commit v3 on v2

--- a/solution.py
+++ b/solution.py
@@ -511,7 +511,6 @@
     low, high = part[:half], part[half:]
     near = halo_near(down, up)
     other = swapped(jnp.where(even, high, low), flip(3, False))
-    near, other = tied(near, other)
     part = jnp.where(even, low, high) + other
     far = halo_far(down, up, near)
     back = band(flipped)
@@ -529,8 +528,6 @@
         part = part + other
         if grad is not None:
             part, grad = tied(part, grad)
-        elif turn == 5 - PIECES:
-            part, far = tied(part, far)
     other = swapped(part, flip(3, False))
     total = jnp.concatenate([jnp.where(even, part, other), jnp.where(even, other, part)], axis=0)
     cells = lax.axis_size("dp") * lax.axis_size("space") * count * S * S

time: 121 us -> 118 us (0.975)
  starting transfers between devices: 45.6 us -> 43.5 us
    ppermute x8, waiting for transfers between devices: 1.99 us -> 0.02 us  [shifted(): return lax.ppermute(value, 'space', pairs)]
    ppermute x8, starting transfers between devices: 21.9 us -> 20.3 us  [swapped(): lax.ppermute(value, AXES, [(number[cell], number[move(cell)]) for cell in...]
    ppermute x8, waiting for transfers between devices: 4.91 us -> 6.52 us  [swapped(): lax.ppermute(value, AXES, [(number[cell], number[move(cell)]) for cell in...]
    unnamed x22 -> x46, local copies, waits for them, and re-layouts: 2.45 us -> 2.5 us
  transfers between devices with their start and end apart: 16 -> 16, of which waited for: 4 -> 5; matrix products, arithmetic and copies ran while one was open for 2% -> 3% of each run, Pallas kernels for 39% -> 39%
where the time goes in v3:
time: 118 us
  Pallas kernels  54.6 us (46%)
  starting transfers between devices  43.5 us (37%)
  local copies, waits for them, and re-layouts  7.56 us (6%)
  waiting for transfers between devices  6.54 us (6%)
  matrix products  2.47 us (2%)
  other arithmetic  1.72 us (1%)
  between operations  1.34 us (1%)
    pallas_call x2, Pallas kernels, forward(): pl.pallas_call(functools.partial(forward_kernel, base), grid_spec=pltpu.P...  31.5 us
    ppermute x8, starting transfers between devices, shifted(): return lax.ppermute(value, 'space', pairs)  23.2 us
    ppermute x8, starting transfers between devices, swapped(): lax.ppermute(value, AXES, [(number[cell], number[move(cell)]) for cell in...  20.3 us
    pallas_call x4, Pallas kernels, backward(): pl.pallas_call(functools.partial(backward_kernel, base), grid_spec=pltpu....  14.8 us
    pallas_call x1, Pallas kernels, edges(): pl.pallas_call(edge_kernel, grid_spec=pltpu.PrefetchScalarGridSpec(num_sc...  8.26 us
    ppermute x8, waiting for transfers between devices, swapped(): lax.ppermute(value, AXES, [(number[cell], number[move(cell)]) for cell in...  6.52 us
    unnamed x46, local copies, waits for them, and re-layouts  2.5 us
    dot_general x12, matrix products, pick(): return jnp.dot(chosen, window[:, lanes], preferred_element_type=F32)  2.47 us
  transfers between devices with their start and end apart: 16, of which 5 were waited for; matrix products, arithmetic and copies ran while one was open for 3% of the time, Pallas kernels for 39%

profile of v3, /device:TPU:1, one launch (start us, length us, event | category | flops | bytes accessed | tf_op | source)
XLA Modules:
  0.0 117.7 jit_solution(9513921998651379391)
XLA Ops:
  0.7 2.0 %fusion.101 = (bf16[32,1,2048]{2,1,0:T(2,128)(2,1)S(1)}, bf16[32,1,2048]{2,1,0:T(2,128)(2,1)S(1)}) fusion(bf16[32,32,2048]{2,1,0:T(8,128)(2,1)} %next_ref.5), kind=kLoop, calls=%fused_computation.174 | loop fusion | bytes 524288 | tf_op jit(solution)/shard_map/slice | solution.py:490
  2.7 0.7 slice_bitcast_fusion
  3.6 4.6 %collective-permute-start = (bf16[32,2176]{1,0:T(8,128)(2,1)S(1)}, bf16[32,2176]{1,0:T(8,128)(2,1)S(1)}, u32[]{:S(2)}, u32[]{:S(2)}) collective-permute-start(bf16[32,2176]{1,0:T(8,128)(2,1)S(1)} %pad_maximum_fusion.10), channel_id=1, source_target_pairs={{0,1},{1,2},{2,3},{3,4},{4,5},{5,6},{6,7},{7,8},{8,9},{9,10},{10,1... | collective-permute-start | bytes 417800 | tf_op jit(solution)/shard_map/ppermute | solution.py:31
  8.2 0.7 pad_maximum_fusion.11
  8.9 1.9 %collective-permute-start.1 = (bf16[32,2176]{1,0:T(8,128)(2,1)}, bf16[32,2176]{1,0:T(8,128)(2,1)S(1)}, u32[]{:S(2)}, u32[]{:S(2)}) collective-permute-start(bf16[32,2176]{1,0:T(8,128)(2,1)} %pad_maximum_fusion.11), channel_id=1, source_target_pairs={{1,0},{2,1},{3,2},{4,3},{5,4},{6,5},{7,6},{8,7},{9,8},{10,9},{11,1... | collective-permute-start | bytes 417800 | tf_op jit(solution)/shard_map/ppermute | solution.py:31
  12.3 15.7 %forward_0.1 = (bf16[32,32,2048]{2,1,0:T(8,128)(2,1)S(1)}, f32[4,16,2304]{2,1,0:T(8,128)S(1)}, f32[2,16,8192]{2,1,0:T(8,128)S(1)}, f32[9,64,64]{2,1,0:T(8,128)S(1)}, f32[64,256]{1,0:T(8,128)S(1)}) custom-call(s32[32,8]{1,0:T(8,128)S(1)} %copy.31.nb_ref, bf16[32,32,2048]{2,1,0:T(8,128)(2,1)} %next_ref.5, bf16[32,32,2048]{2,1,0:T(8,128)(2,1)} %next_ref.5, ...), custom_call_target="tpu_custom_call" | custom-call | flops 17179869184 | bytes 12582912 | tf_op jit(solution)/shard_map/forward_0/pallas_call | solution.py:350
  28.3 3.2 %collective-permute-start.2 = (bf16[64,2176]{1,0:T(8,128)(2,1)S(1)}, bf16[64,2176]{1,0:T(8,128)(2,1)S(1)}, u32[]{:S(2)}, u32[]{:S(2)}) collective-permute-start(bf16[64,2176]{1,0:T(8,128)(2,1)S(1)} %pad_maximum_fusion.6), channel_id=1, source_target_pairs={{0,2},{1,3},{2,4},{3,5},{4,6},{5,7},{6,8},{7,9},{8,10},{9,11},{10,... | collective-permute-start | bytes 835592 | tf_op jit(solution)/shard_map/ppermute | solution.py:31
  31.5 1.3 %collective-permute-start.3 = (bf16[64,2176]{1,0:T(8,128)(2,1)S(1)}, bf16[64,2176]{1,0:T(8,128)(2,1)S(1)}, u32[]{:S(2)}, u32[]{:S(2)}) collective-permute-start(bf16[64,2176]{1,0:T(8,128)(2,1)S(1)} %pad_maximum_fusion.7), channel_id=1, source_target_pairs={{2,0},{3,1},{4,2},{5,3},{6,4},{7,5},{8,6},{9,7},{10,8},{11,9},{12,... | collective-permute-start | bytes 835592 | tf_op jit(solution)/shard_map/ppermute | solution.py:31
  32.8 15.9 %forward_4.1 = (bf16[32,32,2048]{2,1,0:T(8,128)(2,1)S(1)}, f32[4,16,2304]{2,1,0:T(8,128)S(1)}, f32[2,16,8192]{2,1,0:T(8,128)S(1)}, f32[9,64,64]{2,1,0:T(8,128)S(1)}, f32[64,256]{1,0:T(8,128)S(1)}) custom-call(s32[32,8]{1,0:T(8,128)S(1)} %copy.31.nb_ref, bf16[32,32,2048]{2,1,0:T(8,128)(2,1)} %next_ref.5, ...), custom_call_target="tpu_custom_call", output_to_operand_aliasing={{0}: (12, {})} | custom-call | flops 17179869184 | bytes 12582912 | tf_op jit(solution)/shard_map/forward_4/pallas_call | solution.py:350
  48.7 2.0 %copy-done = bf16[32,32,2048]{2,1,0:T(8,128)(2,1)} copy-done((bf16[32,32,2048]{2,1,0:T(8,128)(2,1)}, bf16[32,32,2048]{2,1,0:T(8,128)(2,1)S(1)}, u32[]{:S(2)}) %copy-start) | copy-done | bytes 4194328
  52.2 8.3 %edges.1 = (bf16[32,32,2048]{2,1,0:T(8,128)(2,1)}, bf16[32,2176]{1,0:T(8,128)(2,1)S(1)}, bf16[32,2176]{1,0:T(8,128)(2,1)S(1)}, f32[32,2048]{1,0:T(8,128)S(1)}, f...) custom-call(s32[32,8]{1,0:T(8,128)S(1)} %copy.31.nb_ref, ...), custom_call_target="tpu_custom_call", output_to_operand_aliasing={{0}: (20, {})} | custom-call | flops 8589934592 | bytes 4194304 | tf_op jit(solution)/shard_map/edges/pallas_call | solution.py:394
  60.5 2.7 %collective-permute-start.10 = (bf16[32,2176]{1,0:T(8,128)(2,1)S(1)}, bf16[32,2176]{1,0:T(8,128)(2,1)S(1)}, u32[]{:S(2)}, u32[]{:S(2)}) collective-permute-start(bf16[32,2176]{1,0:T(8,128)(2,1)S(1)} %get-tuple-element.62), channel_id=1, source_target_pairs={{1,0},{2,1},{3,2},{4,3},{5,4},{6,5},{7,6},{8,7},{9,8},{10,9},{11,1... | collective-permute-start | bytes 417800 | tf_op jit(solution)/shard_map/ppermute | solution.py:31
  63.2 4.2 %collective-permute-start.8 = (bf16[32,2176]{1,0:T(8,128)(2,1)S(1)}, bf16[32,2176]{1,0:T(8,128)(2,1)S(1)}, u32[]{:S(2)}, u32[]{:S(2)}) collective-permute-start(bf16[32,2176]{1,0:T(8,128)(2,1)S(1)} %get-tuple-element.61), channel_id=1, source_target_pairs={{0,1},{1,2},{2,3},{3,4},{4,5},{5,6},{6,7},{7,8},{8,9},{9,10},{10,1... | collective-permute-start | bytes 417800 | tf_op jit(solution)/shard_map/ppermute | solution.py:31
  67.8 1.3 %collective-permute-done.4 = f32[208,128]{1,0:T(8,128)S(1)} collective-permute-done((f32[208,128]{1,0:T(8,128)S(1)}, f32[208,128]{1,0:T(8,128)S(1)}, u32[]{:S(2)}, u32[]{:S(2)}) %collective-permute-start.4) | collective-permute-done | bytes 106528 | tf_op jit(solution)/shard_map/ppermute | solution.py:463
  69.2 1.3 %collective-permute-start.5 = (f32[208,128]{1,0:T(8,128)S(1)}, f32[208,128]{1,0:T(8,128)S(1)}, u32[]{:S(2)}, u32[]{:S(2)}) collective-permute-start(f32[208,128]{1,0:T(8,128)S(1)} %select_add_fusion), channel_id=1, source_target_pairs={{0,32},{1,33},{2,34},{3,35},{4,36},{5,37},{6,38},{7,39},{8,40},{9,... | collective-permute-start | bytes 319496 | tf_op jit(solution)/shard_map/ppermute | solution.py:463
  70.5 1.3 %collective-permute-start.11 = (bf16[64,2176]{1,0:T(8,128)(2,1)S(1)}, bf16[64,2176]{1,0:T(8,128)(2,1)S(1)}, u32[]{:S(2)}, u32[]{:S(2)}) collective-permute-start(bf16[64,2176]{1,0:T(8,128)(2,1)S(1)} %pad_maximum_fusion.9), channel_id=1, source_target_pairs={{2,0},{3,1},{4,2},{5,3},{6,4},{7,5},{8,6},{9,7},{10,8},{11,9},{12,... | collective-permute-start | bytes 835592 | tf_op jit(solution)/shard_map/ppermute | solution.py:31
  71.8 4.0 %collective-permute-start.9 = (bf16[64,2176]{1,0:T(8,128)(2,1)S(1)}, bf16[64,2176]{1,0:T(8,128)(2,1)S(1)}, u32[]{:S(2)}, u32[]{:S(2)}) collective-permute-start(bf16[64,2176]{1,0:T(8,128)(2,1)S(1)} %pad_maximum_fusion.8), channel_id=1, source_target_pairs={{0,2},{1,3},{2,4},{3,5},{4,6},{5,7},{6,8},{7,9},{8,10},{9,11},{10,... | collective-permute-start | bytes 835592 | tf_op jit(solution)/shard_map/ppermute | solution.py:31
  75.9 1.9 %collective-permute-start.6 = (f32[208,128]{1,0:T(8,128)S(1)}, f32[208,128]{1,0:T(8,128)S(1)}, u32[]{:S(2)}, u32[]{:S(2)}) collective-permute-start(f32[208,128]{1,0:T(8,128)S(1)} %add.149), channel_id=1, source_target_pairs={{0,96},{1,97},{2,98},{3,99},{4,100},{5,101},{6,102},{7,103},{8,104... | collective-permute-start | bytes 319496 | tf_op jit(solution)/shard_map/ppermute | solution.py:463
  77.9 2.9 %collective-permute-done.6 = f32[208,128]{1,0:T(8,128)S(1)} collective-permute-done((f32[208,128]{1,0:T(8,128)S(1)}, f32[208,128]{1,0:T(8,128)S(1)}, u32[]{:S(2)}, u32[]{:S(2)}) %collective-permute-start.6) | collective-permute-done | bytes 106528 | tf_op jit(solution)/shard_map/ppermute | solution.py:463
  80.8 6.7 %collective-permute-start.7 = (f32[208,128]{1,0:T(8,128)S(1)}, f32[208,128]{1,0:T(8,128)S(1)}, u32[]{:S(2)}, u32[]{:S(2)}) collective-permute-start(f32[208,128]{1,0:T(8,128)S(1)} %add.150), channel_id=1, source_target_pairs={{0,8},{1,9},{2,10},{3,11},{4,12},{5,13},{6,14},{7,15},{8,0},{9,1},... | collective-permute-start | bytes 319496 | tf_op jit(solution)/shard_map/ppermute | solution.py:463
  88.9 3.7 %backward_0.1.rest_0_ = bf16[32,32,2048]{2,1,0:T(8,128)(2,1)} custom-call(s32[32,8]{1,0:T(8,128)S(1)} %copy.31.nb_ref, bf16[32,32,2048]{2,1,0:T(8,128)(2,1)S(1)} %copy-done.1, bf16[32,32,2048]{2,1,0:T(8,128)(2,1)S(1)} %copy-done.1, bf16[32,32,2048]{2,1,0:T(8,128)(2,1)S(1)} %copy-done.1, f32[32,2304]{1,0:T(8,128)S(1)} %pad_maximum_fusion.4.north_ref, ...), custom_call_target="tpu_custom_call" | custom-call | flops 4294967296 | bytes 2097152 | tf_op jit(solution)/shard_map/backward_0/pallas_call | solution.py:440
  92.6 0.6 collective-permute-done.7
  93.3 5.5 %collective-permute-start.12 = (f32[208,128]{1,0:T(8,128)S(1)}, f32[208,128]{1,0:T(8,128)S(1)}, u32[]{:S(2)}, u32[]{:S(2)}) collective-permute-start(f32[208,128]{1,0:T(8,128)S(1)} %add.151), channel_id=1, source_target_pairs={{0,24},{1,25},{2,26},{3,27},{4,28},{5,29},{6,30},{7,31},{8,16},{9,... | collective-permute-start | bytes 319496 | tf_op jit(solution)/shard_map/ppermute | solution.py:463
  98.7 3.7 %backward_2.1.rest_0_ = bf16[32,32,2048]{2,1,0:T(8,128)(2,1)} custom-call(s32[32,8]{1,0:T(8,128)S(1)} %copy.31.nb_ref, bf16[32,32,2048]{2,1,0:T(8,128)(2,1)S(1)} %copy-done.1, bf16[32,32,2048]{2,1,0:T(8,128)(2,1)S(1)} %copy-done.1, bf16[32,32,2048]{2,1,0:T(8,128)(2,1)S(1)} %copy-done.1, ...), custom_call_target="tpu_custom_call", output_to_operand_aliasing={{}: (11, {})} | custom-call | flops 4294967296 | bytes 2097152 | tf_op jit(solution)/shard_map/backward_2/pallas_call | solution.py:440
  102.5 3.7 %backward_4.1.rest_0_ = bf16[32,32,2048]{2,1,0:T(8,128)(2,1)} custom-call(s32[32,8]{1,0:T(8,128)S(1)} %copy.31.nb_ref, bf16[32,32,2048]{2,1,0:T(8,128)(2,1)S(1)} %copy-done.1, bf16[32,32,2048]{2,1,0:T(8,128)(2,1)S(1)} %copy-done.1, bf16[32,32,2048]{2,1,0:T(8,128)(2,1)S(1)} %copy-done.1, ...), custom_call_target="tpu_custom_call", output_to_operand_aliasing={{}: (11, {})} | custom-call | flops 4294967296 | bytes 2097152 | tf_op jit(solution)/shard_map/backward_4/pallas_call | solution.py:440
  106.3 0.4 collective-permute-start.14
  106.6 3.7 %backward_6.1 = bf16[32,32,2048]{2,1,0:T(8,128)(2,1)} custom-call(s32[32,8]{1,0:T(8,128)S(1)} %copy.31.nb_ref, bf16[32,32,2048]{2,1,0:T(8,128)(2,1)S(1)} %copy-done.1, bf16[32,32,2048]{2,1,0:T(8,128)(2,1)S(1)} %copy-done.1, bf16[32,32,2048]{2,1,0:T(8,128)(2,1)S(1)} %copy-done.1, ...), custom_call_target="tpu_custom_call", output_to_operand_aliasing={{}: (11, {})} | custom-call | flops 4294967296 | bytes 2097152 | tf_op jit(solution)/shard_map/backward_6/pallas_call | solution.py:440
  110.3 0.8 collective-permute-done.14
  111.1 4.2 %collective-permute-start.15 = (f32[208,128]{1,0:T(8,128)S(1)}, f32[208,128]{1,0:T(8,128)S(1)}, u32[]{:S(2)}, u32[]{:S(2)}) collective-permute-start(f32[208,128]{1,0:T(8,128)S(1)} %add.154), channel_id=1, source_target_pairs={{0,1},{1,0},{2,3},{3,2},{4,5},{5,4},{6,7},{7,6},{8,9},{9,8},{10,11... | collective-permute-start | bytes 319496 | tf_op jit(solution)/shard_map/ppermute | solution.py:463
  115.3 1.0 collective-permute-done.15
  116.4 0.7 reshape.64
  117.1 0.6 reshape.65
  (116 shorter events, 5.3 us)
Async XLA Ops:
  0.6 10.2 %copy-start.2 = (bf16[9,4096]{1,0:T(8,128)(2,1)S(1)}, bf16[9,4096]{1,0:T(8,128)(2,1)}, u32[]{:S(2)}) copy-start(bf16[9,4096]{1,0:T(8,128)(2,1)} %param.10) | copy-start | bytes 221188
  0.6 10.6 %copy-start.4 = (s32[32,8]{0,1:T(8,128)S(1)}, s32[32,8]{0,1:T(8,128)}, u32[]{:S(2)}) copy-start(s32[32,8]{0,1:T(8,128)} %param.9) | copy-start | bytes 3076
  0.7 10.8 %copy-start.17 = (f32[64]{0:T(128)S(1)}, f32[64]{0:T(128)}, u32[]{:S(2)}) copy-start(f32[64]{0:T(128)} %param.12) | copy-start | bytes 772
  2.7 9.1 %copy-start.3 = (bf16[64,256]{1,0:T(8,128)(2,1)S(1)}, bf16[64,256]{1,0:T(8,128)(2,1)}, u32[]{:S(2)}) copy-start(bf16[64,256]{1,0:T(8,128)(2,1)} %param.11) | copy-start | bytes 98308
  3.6 24.7 %collective-permute-start = (bf16[32,2176]{1,0:T(8,128)(2,1)S(1)}, bf16[32,2176]{1,0:T(8,128)(2,1)S(1)}, u32[]{:S(2)}, u32[]{:S(2)}) collective-permute-start(bf16[32,2176]{1,0:T(8,128)(2,1)S(1)} %pad_maximum_fusion.10), channel_id=1, source_target_pairs={{0,1},{1,2},{2,3},{3,4},{4,5},{5,6},{6,7},{7,8},{8,9},{9,10},{10,1... | collective-permute-start | bytes 417800 | tf_op jit(solution)/shard_map/ppermute | solution.py:31
  8.9 19.3 %collective-permute-start.1 = (bf16[32,2176]{1,0:T(8,128)(2,1)}, bf16[32,2176]{1,0:T(8,128)(2,1)S(1)}, u32[]{:S(2)}, u32[]{:S(2)}) collective-permute-start(bf16[32,2176]{1,0:T(8,128)(2,1)} %pad_maximum_fusion.11), channel_id=1, source_target_pairs={{1,0},{2,1},{3,2},{4,3},{5,4},{6,5},{7,6},{8,7},{9,8},{10,9},{11,1... | collective-permute-start | bytes 417800 | tf_op jit(solution)/shard_map/ppermute | solution.py:31
  11.4 39.4 %copy-start.15 = (s32[32]{0:T(128)}, s32[32]{0:T(128)S(1)}, u32[]{:S(2)}) copy-start(s32[32]{0:T(128)S(1)} %get-tuple-element.87) | copy-start | bytes 388
  11.4 39.6 %copy-start.13 = (s32[32]{0:T(128)}, s32[32]{0:T(128)S(1)}, u32[]{:S(2)}) copy-start(s32[32]{0:T(128)S(1)} %get-tuple-element.91) | copy-start | bytes 388
  11.4 39.9 %copy-start.11 = (s32[32]{0:T(128)}, s32[32]{0:T(128)S(1)}, u32[]{:S(2)}) copy-start(s32[32]{0:T(128)S(1)} %get-tuple-element.90) | copy-start | bytes 388
  11.4 40.0 %copy-start.9 = (s32[32]{0:T(128)}, s32[32]{0:T(128)S(1)}, u32[]{:S(2)}) copy-start(s32[32]{0:T(128)S(1)} %get-tuple-element.88) | copy-start | bytes 388
  11.4 40.2 %copy-start.7 = (s32[32]{0:T(128)}, s32[32]{0:T(128)S(1)}, u32[]{:S(2)}) copy-start(s32[32]{0:T(128)S(1)} %get-tuple-element.92) | copy-start | bytes 388
  11.4 40.5 %copy-start.5 = (s32[32]{0:T(128)}, s32[32]{0:T(128)S(1)}, u32[]{:S(2)}) copy-start(s32[32]{0:T(128)S(1)} %get-tuple-element.89) | copy-start | bytes 388
  28.3 22.5 %collective-permute-start.2 = (bf16[64,2176]{1,0:T(8,128)(2,1)S(1)}, bf16[64,2176]{1,0:T(8,128)(2,1)S(1)}, u32[]{:S(2)}, u32[]{:S(2)}) collective-permute-start(bf16[64,2176]{1,0:T(8,128)(2,1)S(1)} %pad_maximum_fusion.6), channel_id=1, source_target_pairs={{0,2},{1,3},{2,4},{3,5},{4,6},{5,7},{6,8},{7,9},{8,10},{9,11},{10,... | collective-permute-start | bytes 835592 | tf_op jit(solution)/shard_map/ppermute | solution.py:31
  31.5 19.2 %collective-permute-start.3 = (bf16[64,2176]{1,0:T(8,128)(2,1)S(1)}, bf16[64,2176]{1,0:T(8,128)(2,1)S(1)}, u32[]{:S(2)}, u32[]{:S(2)}) collective-permute-start(bf16[64,2176]{1,0:T(8,128)(2,1)S(1)} %pad_maximum_fusion.7), channel_id=1, source_target_pairs={{2,0},{3,1},{4,2},{5,3},{6,4},{7,5},{8,6},{9,7},{10,8},{11,9},{12,... | collective-permute-start | bytes 835592 | tf_op jit(solution)/shard_map/ppermute | solution.py:31
  60.5 10.0 %collective-permute-start.10 = (bf16[32,2176]{1,0:T(8,128)(2,1)S(1)}, bf16[32,2176]{1,0:T(8,128)(2,1)S(1)}, u32[]{:S(2)}, u32[]{:S(2)}) collective-permute-start(bf16[32,2176]{1,0:T(8,128)(2,1)S(1)} %get-tuple-element.62), channel_id=1, source_target_pairs={{1,0},{2,1},{3,2},{4,3},{5,4},{6,5},{7,6},{8,7},{9,8},{10,9},{11,1... | collective-permute-start | bytes 417800 | tf_op jit(solution)/shard_map/ppermute | solution.py:31
  63.2 8.6 %collective-permute-start.8 = (bf16[32,2176]{1,0:T(8,128)(2,1)S(1)}, bf16[32,2176]{1,0:T(8,128)(2,1)S(1)}, u32[]{:S(2)}, u32[]{:S(2)}) collective-permute-start(bf16[32,2176]{1,0:T(8,128)(2,1)S(1)} %get-tuple-element.61), channel_id=1, source_target_pairs={{0,1},{1,2},{2,3},{3,4},{4,5},{5,6},{6,7},{7,8},{8,9},{9,10},{10,1... | collective-permute-start | bytes 417800 | tf_op jit(solution)/shard_map/ppermute | solution.py:31
  67.6 1.6 %collective-permute-start.4 = (f32[208,128]{1,0:T(8,128)S(1)}, f32[208,128]{1,0:T(8,128)S(1)}, u32[]{:S(2)}, u32[]{:S(2)}) collective-permute-start(f32[208,128]{1,0:T(8,128)S(1)} %slice_select_fusion), channel_id=1, source_target_pairs={{0,1},{1,0},{2,3},{3,2},{4,5},{5,4},{6,7},{7,6},{8,9},{9,8},{10,11... | collective-permute-start | bytes 319496 | tf_op jit(solution)/shard_map/ppermute | solution.py:463
  69.2 18.4 %copy-start.16 = (s32[32]{0:T(128)S(1)}, s32[32]{0:T(128)}, u32[]{:S(2)}) copy-start(s32[32]{0:T(128)} %copy-done.15) | copy-start | bytes 388
  69.2 18.6 %copy-start.14 = (s32[32]{0:T(128)S(1)}, s32[32]{0:T(128)}, u32[]{:S(2)}) copy-start(s32[32]{0:T(128)} %copy-done.13) | copy-start | bytes 388
  69.2 18.8 %copy-start.8 = (s32[32]{0:T(128)S(1)}, s32[32]{0:T(128)}, u32[]{:S(2)}) copy-start(s32[32]{0:T(128)} %copy-done.7) | copy-start | bytes 388
  69.2 6.7 %collective-permute-start.5 = (f32[208,128]{1,0:T(8,128)S(1)}, f32[208,128]{1,0:T(8,128)S(1)}, u32[]{:S(2)}, u32[]{:S(2)}) collective-permute-start(f32[208,128]{1,0:T(8,128)S(1)} %select_add_fusion), channel_id=1, source_target_pairs={{0,32},{1,33},{2,34},{3,35},{4,36},{5,37},{6,38},{7,39},{8,40},{9,... | collective-permute-start | bytes 319496 | tf_op jit(solution)/shard_map/ppermute | solution.py:463
  70.5 17.0 %collective-permute-start.11 = (bf16[64,2176]{1,0:T(8,128)(2,1)S(1)}, bf16[64,2176]{1,0:T(8,128)(2,1)S(1)}, u32[]{:S(2)}, u32[]{:S(2)}) collective-permute-start(bf16[64,2176]{1,0:T(8,128)(2,1)S(1)} %pad_maximum_fusion.9), channel_id=1, source_target_pairs={{2,0},{3,1},{4,2},{5,3},{6,4},{7,5},{8,6},{9,7},{10,8},{11,9},{12,... | collective-permute-start | bytes 835592 | tf_op jit(solution)/shard_map/ppermute | solution.py:31
  71.8 16.4 %copy-start.6 = (s32[32]{0:T(128)S(1)}, s32[32]{0:T(128)}, u32[]{:S(2)}) copy-start(s32[32]{0:T(128)} %copy-done.5) | copy-start | bytes 388
  71.8 16.3 %collective-permute-start.9 = (bf16[64,2176]{1,0:T(8,128)(2,1)S(1)}, bf16[64,2176]{1,0:T(8,128)(2,1)S(1)}, u32[]{:S(2)}, u32[]{:S(2)}) collective-permute-start(bf16[64,2176]{1,0:T(8,128)(2,1)S(1)} %pad_maximum_fusion.8), channel_id=1, source_target_pairs={{0,2},{1,3},{2,4},{3,5},{4,6},{5,7},{6,8},{7,9},{8,10},{9,11},{10,... | collective-permute-start | bytes 835592 | tf_op jit(solution)/shard_map/ppermute | solution.py:31
  75.9 4.8 %collective-permute-start.6 = (f32[208,128]{1,0:T(8,128)S(1)}, f32[208,128]{1,0:T(8,128)S(1)}, u32[]{:S(2)}, u32[]{:S(2)}) collective-permute-start(f32[208,128]{1,0:T(8,128)S(1)} %add.149), channel_id=1, source_target_pairs={{0,96},{1,97},{2,98},{3,99},{4,100},{5,101},{6,102},{7,103},{8,104... | collective-permute-start | bytes 319496 | tf_op jit(solution)/shard_map/ppermute | solution.py:463
  77.8 10.7 %copy-start.12 = (s32[32]{0:T(128)S(1)}, s32[32]{0:T(128)}, u32[]{:S(2)}) copy-start(s32[32]{0:T(128)} %copy-done.11) | copy-start | bytes 388
  77.8 10.8 %copy-start.10 = (s32[32]{0:T(128)S(1)}, s32[32]{0:T(128)}, u32[]{:S(2)}) copy-start(s32[32]{0:T(128)} %copy-done.9) | copy-start | bytes 388
  80.8 12.5 %collective-permute-start.7 = (f32[208,128]{1,0:T(8,128)S(1)}, f32[208,128]{1,0:T(8,128)S(1)}, u32[]{:S(2)}, u32[]{:S(2)}) collective-permute-start(f32[208,128]{1,0:T(8,128)S(1)} %add.150), channel_id=1, source_target_pairs={{0,8},{1,9},{2,10},{3,11},{4,12},{5,13},{6,14},{7,15},{8,0},{9,1},... | collective-permute-start | bytes 319496 | tf_op jit(solution)/shard_map/ppermute | solution.py:463
  93.3 9.2 %collective-permute-start.12 = (f32[208,128]{1,0:T(8,128)S(1)}, f32[208,128]{1,0:T(8,128)S(1)}, u32[]{:S(2)}, u32[]{:S(2)}) collective-permute-start(f32[208,128]{1,0:T(8,128)S(1)} %add.151), channel_id=1, source_target_pairs={{0,24},{1,25},{2,26},{3,27},{4,28},{5,29},{6,30},{7,31},{8,16},{9,... | collective-permute-start | bytes 319496 | tf_op jit(solution)/shard_map/ppermute | solution.py:463
  102.4 3.8 %collective-permute-start.13 = (f32[208,128]{1,0:T(8,128)S(1)}, f32[208,128]{1,0:T(8,128)S(1)}, u32[]{:S(2)}, u32[]{:S(2)}) collective-permute-start(f32[208,128]{1,0:T(8,128)S(1)} %add.152), channel_id=1, source_target_pairs={{0,2},{1,3},{2,0},{3,1},{4,6},{5,7},{6,4},{7,5},{8,10},{9,11},{10,... | collective-permute-start | bytes 319496 | tf_op jit(solution)/shard_map/ppermute | solution.py:463
  106.3 4.8 %collective-permute-start.14 = (f32[208,128]{1,0:T(8,128)S(1)}, f32[208,128]{1,0:T(8,128)S(1)}, u32[]{:S(2)}, u32[]{:S(2)}) collective-permute-start(f32[208,128]{1,0:T(8,128)S(1)} %add.153), channel_id=1, source_target_pairs={{0,6},{1,7},{2,4},{3,5},{4,2},{5,3},{6,0},{7,1},{8,14},{9,15},{10,... | collective-permute-start | bytes 319496 | tf_op jit(solution)/shard_map/ppermute | solution.py:463
  111.1 5.1 %collective-permute-start.15 = (f32[208,128]{1,0:T(8,128)S(1)}, f32[208,128]{1,0:T(8,128)S(1)}, u32[]{:S(2)}, u32[]{:S(2)}) collective-permute-start(f32[208,128]{1,0:T(8,128)S(1)} %add.154), channel_id=1, source_target_pairs={{0,1},{1,0},{2,3},{3,2},{4,5},{5,4},{6,7},{7,6},{8,9},{9,8},{10,11... | collective-permute-start | bytes 319496 | tf_op jit(solution)/shard_map/ppermute | solution.py:463
  (3 other events, 18.7 us)
